TPU v7x, 32 devices: a whole 2x2x4 slice. The times are simulated.
32 devices in a mesh: lat: 8 (over z, x), lon: 4 (over y, core).
Axes of the slice: x: 2, y: 2, z: 4, core: 2. Of those that a mesh axis runs over, the one named last changes fastest.
Arguments:
- spectra: bfloat16 [32768, 8448], P(('lat', 'lon')), may hold values from -6 to 6
- pc_basis: bfloat16 [8448, 256], replicated, may hold values from -0.0625 to 0.0625
- destination: int32 [32768, 1], P(('lat', 'lon')), may hold values from 0 to 31; in each aligned block of 1024 rows (0 to 1023, 1024 to 2047, ...) at most 64 rows name the same one
- corner_row: int32 [32768], P(('lat', 'lon')), may hold values from 0 to 64
- corner_col: int32 [32768], P(('lat', 'lon')), may hold values from 0 to 64
- corner_weight: bfloat16 [32768, 4], P(('lat', 'lon')), may hold values from 0 to 1
- state: bfloat16 [512, 256, 128], P('lat', 'lon'), may hold values from -6 to 6
- inv_sigma: float32 [256], replicated, may hold values from 0.5 to 2
- w_in: bfloat16 [128, 512], replicated, may hold values from -0.5 to 0.5
- b_in: float32 [512], replicated, may hold values from -3 to 3
- w_out: bfloat16 [512, 256], replicated, may hold values from -0.25 to 0.25
- b_out: float32 [256], replicated, may hold values from -3 to 3
Outputs:
- departures: bfloat16 [32768, 256], P(('lat', 'lon'))
- state_gradient: float32 [512, 256, 128], P('lat', 'lon')
Inputs may be any that keep to these rules, and one draw needn't show every extreme that they name: `destination`: in the rows of one device no tile is named by more than 64 spectra, a bound that some block reaches.
All inputs are finite; a program needn't handle non-finite values.
Results may differ from a plain program's by a relative error of at most 0.0075.
Values may be sent and summed in bfloat16 or wider, within the bound.
A program may use at most 128 MiB of HBM per device.

v0:
```python
import jax
import jax.numpy as jnp
from jax import lax
from jax.sharding import PartitionSpec as P


def padded(cells, sides, width, closed):
    for axis, dim in sides:
        count = lax.axis_size(axis)
        ends = count if closed else count - 1
        head = lax.slice_in_dim(cells, 0, width, axis=dim)
        tail = lax.slice_in_dim(cells, cells.shape[dim] - width, cells.shape[dim], axis=dim)
        cells = jnp.concatenate(
            [
                lax.ppermute(tail, axis, [(i, (i + 1) % count) for i in range(ends)]),
                cells,
                lax.ppermute(head, axis, [((i + 1) % count, i) for i in range(ends)]),
            ],
            axis=dim,
        )
    return cells


def per_device(
    spectra,
    pc_basis,
    destination,
    corner_row,
    corner_col,
    corner_weight,
    state,
    inv_sigma,
    w_in,
    b_in,
    w_out,
    b_out,
):
    pcs = jnp.dot(spectra, pc_basis, preferred_element_type=jnp.float32).astype(jnp.bfloat16)
    n_lat = lax.axis_size("lat")
    n_lon = lax.axis_size("lon")
    devices = n_lat * n_lon
    obs_rows = spectra.shape[0]
    capacity = max(2, 2 * obs_rows // devices)
    dest = destination[:, 0]
    onehot = (dest[:, None] == jnp.arange(devices, dtype=jnp.int32)[None, :]).astype(jnp.int32)
    slot = jnp.sum(jnp.cumsum(onehot, 0) * onehot, 1) - 1
    place = dest * capacity + slot
    extra = jnp.zeros((obs_rows, 2), jnp.bfloat16)
    meta = jnp.concatenate(
        [
            corner_weight,
            corner_row[:, None].astype(jnp.bfloat16),
            corner_col[:, None].astype(jnp.bfloat16),
            extra,
        ],
        1,
    )
    send_meta = jnp.zeros((devices * capacity, 8), jnp.bfloat16).at[place].set(meta)
    recv_meta = lax.all_to_all(
        send_meta.reshape(devices, capacity, 8),
        ("lat", "lon"),
        split_axis=0,
        concat_axis=0,
        tiled=True,
    )
    recv_meta = recv_meta.reshape(devices * capacity, 8)
    tile_rows, tile_cols, levels = state.shape
    extended = padded(state, (("lat", 0),), 1, False)
    extended = padded(extended, (("lon", 1),), 1, True)
    width = tile_cols + 2
    cells = (tile_rows + 2) * width
    flat = extended.reshape(cells, levels)
    base_row = recv_meta[:, 4].astype(jnp.int32)
    base_col = recv_meta[:, 5].astype(jnp.int32)
    offsets = [(0, 0), (1, 0), (0, 1), (1, 1)]
    indices = [(base_row + offsets[k][0]) * width + base_col + offsets[k][1] for k in range(4)]
    slots = recv_meta.shape[0]
    cells_pad = -(-cells // 128) * 128
    cell_ids = jnp.arange(cells_pad, dtype=jnp.int32)[None, :]
    weights_low = recv_meta[:, 0:4]
    matrix = jnp.zeros((slots, cells_pad), jnp.bfloat16)
    for k in range(4):
        matrix = matrix + jnp.where(
            indices[k][:, None] == cell_ids, weights_low[:, k : k + 1], jnp.zeros((), jnp.bfloat16)
        )
    flat_pad = jnp.pad(flat, ((0, cells_pad - cells), (0, 0)))
    column = jnp.dot(matrix, flat_pad, preferred_element_type=jnp.float32).astype(jnp.bfloat16)
    pulled = lax.all_to_all(
        column.reshape(devices, capacity, levels),
        ("lat", "lon"),
        split_axis=0,
        concat_axis=0,
        tiled=True,
    )
    net_column = pulled.reshape(devices * capacity, levels)[place]
    pre = jnp.dot(net_column, w_in, preferred_element_type=jnp.float32) + b_in
    hidden = jax.nn.silu(pre).astype(jnp.bfloat16)
    sim = jnp.dot(hidden, w_out, preferred_element_type=jnp.float32) + b_out
    dep = (sim - pcs.astype(jnp.float32)) * inv_sigma
    dep_out = dep.astype(jnp.bfloat16)
    g_sim = (dep * inv_sigma).astype(jnp.bfloat16)
    g_hidden = lax.dot_general(
        g_sim, w_out, (((1,), (1,)), ((), ())), preferred_element_type=jnp.float32
    )
    sig = jax.nn.sigmoid(pre)
    g_pre = (g_hidden * sig * (1.0 + pre * (1.0 - sig))).astype(jnp.bfloat16)
    g_column = lax.dot_general(
        g_pre, w_in, (((1,), (1,)), ((), ())), preferred_element_type=jnp.float32
    )
    send_grad = jnp.zeros((devices * capacity, levels), jnp.float32).at[place].set(g_column)
    g_owner = lax.all_to_all(
        send_grad.reshape(devices, capacity, levels).astype(jnp.bfloat16),
        ("lat", "lon"),
        split_axis=0,
        concat_axis=0,
        tiled=True,
    ).astype(jnp.float32)
    g_owner = g_owner.reshape(devices * capacity, levels)
    g_flat = lax.dot_general(
        matrix.astype(jnp.float32),
        g_owner,
        (((0,), (0,)), ((), ())),
        precision=lax.Precision.HIGHEST,
    )[:cells]
    g_ext = g_flat.reshape(tile_rows + 2, width, levels)
    col_pad = padded(g_ext.astype(jnp.bfloat16), (("lon", 1),), 1, True).astype(g_ext.dtype)
    g_cols = g_ext[:, 1 : tile_cols + 1]
    g_cols = g_cols.at[:, 0].add(col_pad[:, 0]).at[:, tile_cols - 1].add(col_pad[:, tile_cols + 3])
    row_pad = padded(g_cols.astype(jnp.bfloat16), (("lat", 0),), 1, False).astype(g_cols.dtype)
    gradient = g_cols[1 : tile_rows + 1]
    gradient = gradient.at[0].add(row_pad[0]).at[tile_rows - 1].add(row_pad[tile_rows + 3])
    return (dep_out, gradient)


def solution(mesh):
    return jax.shard_map(
        per_device,
        mesh=mesh,
        in_specs=(
            P(("lat", "lon"), None),
            P(),
            P(("lat", "lon"), None),
            P(("lat", "lon")),
            P(("lat", "lon")),
            P(("lat", "lon"), None),
            P("lat", "lon", None),
            P(),
            P(),
            P(),
            P(),
            P(),
        ),
        out_specs=(P(("lat", "lon"), None), P("lat", "lon", None)),
        check_vma=False,
    )
```

profile of v0, /device:TPU:0, one launch (start us, length us, event | category | flops | bytes accessed | tf_op | source)
XLA Modules:
  0.0 163.0 jit_solution(8227532038127725734)
XLA Ops:
  0.7 0.8 fusion.36
  1.5 4.8 %collective-permute-start = (bf16[1,64,128]{2,1,0:T(8,128)(2,1)S(1)}, bf16[1,64,128]{2,1,0:T(8,128)(2,1)S(1)}, u32[]{:S(2)}, u32[]{:S(2)}) collective-permute-start(bf16[1,64,128]{2,1,0:T(8,128)(2,1)S(1)} %get-tuple-element.65), channel_id=1, source_target_pairs={{0,4},{4,8},{8,12},{12,16},{16,20},{20,24},{24,28},{1,5},{5,9},{9,... | collective-permute-start | bytes 49160 | tf_op jit(solution)/shard_map/ppermute | solution.py:15
  6.3 0.7 fusion.25
  7.0 9.0 %reduce-window.6 = s32[32,8,128]{2,1,0:T(8,128)S(1)} reduce-window(s32[32,8,128]{2,1,0:T(8,128)S(1)} %fusion.25, s32[]{:T(128)} %constant.126.clone.1), window={size=1x1x128 pad=0_0x0_0x127_0}, to_apply=%region_0.0 | reduce-window | flops 4161536 | bytes 262148 | tf_op jit(solution)/shard_map/reduce-window
  16.5 0.7 fusion.24
  17.2 0.7 convert_element_type.77
  17.9 0.7 convert_element_type.75
  18.7 0.8 maximum_maximum_fusion
  19.5 0.7 compare_select_fusion
  20.2 0.2 copy.24
  20.4 3.3 %scatter_custom_fusion = bf16[2048,8]{1,0:T(8,128)(2,1)S(1)} fusion(s32[1024]{0:T(1024)S(1)} %bitcast.54, bf16[1024,8]{1,0:T(8,128)(2,1)S(1)} %copy.24, bf16[]{:T(256)} %constant.124.clone.1), kind=kCustom, calls=%fused_computation.35 | custom fusion | bytes 32770 | tf_op jit(solution)/shard_map/scatter | solution.py:58
  23.7 0.2 copy.25
  23.9 0.7 reshape.210
  24.7 4.9 %all-to-all-start = ((bf16[32,2,256]{2,1,0:T(2,128)(2,1)}), bf16[32,2,256]{2,1,0:T(2,128)(2,1)S(1)}, u32[]{:S(2)}, u32[]{:S(2)}) async-start(bf16[32,2,256]{2,1,0:T(2,128)(2,1)} %reshape.210), calls=%async_computation | async-start | bytes 65536 | tf_op jit(solution)/shard_map/all_to_all | solution.py:59
  29.6 1.3 collective-permute-start.1
  31.1 4.2 %collective-permute-done.1 = bf16[1,64,128]{2,1,0:T(8,128)(2,1)S(1)} collective-permute-done((bf16[1,64,128]{2,1,0:T(8,128)(2,1)S(1)}, bf16[1,64,128]{2,1,0:T(8,128)(2,1)S(1)}, u32[]{:S(2)}, u32[]{:S(2)}) %collective-permute-start.1) | collective-permute-done | bytes 16416 | tf_op jit(solution)/shard_map/ppermute | solution.py:17
  35.3 0.7 collective-permute-start.3
  36.0 1.6 collective-permute-done.3
  37.6 1.8 %collective-permute-done.2 = bf16[66,1,128]{2,1,0:T(2,128)(2,1)S(1)} collective-permute-done((bf16[66,1,128]{2,1,0:T(2,128)(2,1)S(1)}, bf16[66,1,128]{2,1,0:T(2,128)(2,1)S(1)}, u32[]{:S(2)}, u32[]{:S(2)}) %collective-permute-start.2) | collective-permute-done | bytes 16928 | tf_op jit(solution)/shard_map/ppermute | solution.py:15
  39.4 0.6 pad_maximum_fusion
  40.0 0.3 reshape.173
  40.8 30.2 %fusion.4 = bf16[2048,4480]{1,0:T(8,128)(2,1)S(1)} fusion(s32[2048]{0:T(1024)S(1)} %bitcast.51, s32[2048]{0:T(1024)S(1)} %bitcast.49, s32[2048]{0:T(1024)S(1)} %bitcast.52, s32[2048]{0:T(1024)S(1)} %bitcast.50, bf16[2048]{0:T(1024)(128)(2,1)S(1)} %get-tuple-element.51, bf16[2048]{0:T(1024)(128)(2,1)S(1)} %get-tuple-element.52, ...), kind=kLoop, calls=%fused_computation.11 | loop fusion | flops 146800640 | bytes 18399232 | tf_op jit(solution)/shard_map/add | solution.py:83
  71.0 6.8 %convolution_convert_fusion = bf16[2048,128]{1,0:T(8,128)(2,1)} fusion(bf16[2048,4480]{1,0:T(8,128)(2,1)S(1)} %fusion.4, bf16[4356,128]{1,0:T(8,128)(2,1)S(1)} %reshape.173), kind=kOutput, calls=%fused_computation.16 | convolution fusion | flops 2349072384 | bytes 19989504 | tf_op jit(solution)/shard_map/dot_general | solution.py:87
  77.8 5.3 %all-to-all-start.1 = ((bf16[32,64,128]{2,1,0:T(8,128)(2,1)}), bf16[32,64,128]{2,1,0:T(8,128)(2,1)S(1)}, u32[]{:S(2)}, u32[]{:S(2)}) async-start(bf16[32,64,128]{2,1,0:T(8,128)(2,1)} %bitcast.11), calls=%async_computation.1 | async-start | bytes 1048576 | tf_op jit(solution)/shard_map/all_to_all | solution.py:88
  83.1 12.7 %fusion.11 = f32[1024,256]{1,0:T(8,128)} fusion(bf16[1024,8448]{1,0:T(8,128)(2,1)} %param.20, bf16[8448,256]{1,0:T(8,128)(2,1)} %param.21), kind=kOutput, calls=%fused_computation.24 | convolution fusion | flops 4429709312 | bytes 22675456 | tf_op jit(solution)/shard_map/dot_general | solution.py:38
  95.9 2.6 %all-to-all-done.1 = bf16[32,64,128]{2,1,0:T(8,128)(2,1)S(1)} async-done(((bf16[32,64,128]{2,1,0:T(8,128)(2,1)}), bf16[32,64,128]{2,1,0:T(8,128)(2,1)S(1)}, u32[]{:S(2)}, u32[]{:S(2)}) %all-to-all-start.1) | async-done | bytes 524320 | tf_op jit(solution)/shard_map/all_to_all | solution.py:88
  98.5 3.2 %gather_fusion = bf16[1024,128]{1,0:T(8,128)(2,1)S(1)} fusion(bf16[2048,128]{1,0:T(8,128)(2,1)S(1)} %bitcast.40, s32[1024]{0:T(1024)S(1)} %broadcast_clamp_fusion), kind=kCustom, calls=%fused_computation | custom fusion | bytes 528384 | tf_op jit(solution)/shard_map/gather | solution.py:95
  101.7 0.4 fusion.38
  102.2 0.8 copy-done.10
  102.9 1.9 %fusion.37 = (bf16[1024,256]{1,0:T(8,128)(2,1)}, f32[1024,256]{1,0:T(8,128)}) fusion(f32[256]{0:T(256)S(1)} %copy-done.9, f32[1024,256]{1,0:T(8,128)S(1)} %copy-done.10, f32[256]{0:T(256)S(1)} %copy-done.8, bf16[512,256]{1,0:T(8,128)(2,1)S(1)} %copy-done, f32[1024,512]{1,0:T(8,128)S(1)} %fusion.38, f32[512]{0:T(512)S(1)} %copy-done.7), kind=kOutput, calls=%fused_computation.79 | convolution fusion | flops 272629760 | bytes 4984832 | tf_op jit(solution)/shard_map/dot_general | solution.py:98
  104.8 2.3 %fusion.12 = f32[1024,128]{1,0:T(8,128)S(1)} fusion(bf16[128,512]{1,0:T(8,128)(2,1)S(1)} %copy-done.6, f32[1024,512]{1,0:T(8,128)S(1)} %fusion.38, bf16[512,256]{1,0:T(8,128)(2,1)S(1)} %copy-done, f32[512]{0:T(512)S(1)} %copy-done.7, f32[1024,256]{1,0:T(8,128)} %get-tuple-element.69, f32[256]{0:T(256)S(1)} %copy-done.9), kind=kOutput, calls=%fused_computation.25 | convolution fusion | flops 408420352 | bytes 4066304 | tf_op jit(solution)/shard_map/dot_general | solution.py:107
  107.1 3.3 %scatter_custom_fusion.1 = f32[2048,128]{1,0:T(8,128)S(1)} fusion(s32[1024]{0:T(1024)S(1)} %bitcast.56, f32[1024,128]{1,0:T(8,128)S(1)} %fusion.12, f32[]{:T(128)} %constant.132.clone.1), kind=kCustom, calls=%fused_computation.32 | custom fusion | bytes 1048580 | tf_op jit(solution)/shard_map/scatter | solution.py:110
  110.5 18.4 %all_to_all.15 = bf16[32,64,128]{2,1,0:T(8,128)(2,1)S(1)} all-to-all(bf16[32,64,128]{2,1,0:T(8,128)(2,1)S(1)} %bitcast.41), channel_id=1, replica_groups=mesh['lat'=8,'lon'=4] {'lat','lon'}, dimensions={0} | all-to-all | bytes 1048576 | tf_op jit(solution)/shard_map/all_to_all | solution.py:111
  129.0 10.2 %fusion.7 = f32[4356,128]{1,0:T(8,128)} fusion(bf16[2048,128]{1,0:T(8,128)(2,1)S(1)} %bitcast.43, bf16[2048,4480]{1,0:T(8,128)(2,1)} %copy-done.2), kind=kOutput, calls=%fused_computation.14 | convolution fusion | flops 2283798528 | bytes 21104640 | tf_op jit(solution)/shard_map/dot_general | solution.py:119
  139.1 2.3 %reshape.177 = f32[66,66,128]{2,1,0:T(8,128)S(1)} reshape(f32[4356,128]{1,0:T(8,128)} %fusion.7) | data formatting | bytes 4460544 | tf_op jit(solution)/shard_map/reshape | solution.py:125
  141.4 0.2 convert_element_type.90
  141.6 1.0 collective-permute-start.5
  142.6 1.7 %slice.205 = f32[66,64,128]{2,1,0:T(8,128)} slice(f32[66,66,128]{2,1,0:T(8,128)S(1)} %reshape.177), slice={[0:66], [1:65], [0:128]} | slice | bytes 4325376 | tf_op jit(solution)/shard_map/slice | solution.py:127
  144.4 1.6 collective-permute-done.4
  146.1 2.6 %scatter-add.14 = f32[66,64,128]{2,1,0:T(8,128)} dynamic-update-slice(f32[66,64,128]{2,1,0:T(8,128)} %slice.205, f32[66,1,128]{2,1,0:T(1,128)S(1)} %convert_add_fusion, s32[]{:T(128)} %constant.126.clone.1, s32[]{:T(128)} %constant.126.clone.1, s32[]{:T(128)} %constant.126.clone.1) | dynamic-update-slice | bytes 67588 | tf_op jit(solution)/shard_map/scatter-add | solution.py:128
  148.7 1.1 fusion.27
  149.8 2.6 %scatter-add.15 = f32[66,64,128]{2,1,0:T(8,128)} dynamic-update-slice(f32[66,64,128]{2,1,0:T(8,128)} %scatter-add.14, f32[66,1,128]{2,1,0:T(1,128)S(1)} %fusion.27, s32[]{:T(128)} %constant.126.clone.1, s32[]{:T(128)} %constant.133.clone.1, s32[]{:T(128)} %constant.126.clone.1) | dynamic-update-slice | bytes 67588 | tf_op jit(solution)/shard_map/scatter-add | solution.py:128
  152.4 2.0 %convert_element_type.92 = bf16[66,64,128]{2,1,0:T(8,128)(2,1)S(1)} convert(f32[66,64,128]{2,1,0:T(8,128)} %scatter-add.15) | non-fusion elementwise | flops 540672 | bytes 3244032 | tf_op jit(solution)/shard_map/convert_element_type | solution.py:129
  154.4 1.3 collective-permute-start.7
  155.7 4.5 %collective-permute-start.6 = (bf16[1,64,128]{2,1,0:T(8,128)(2,1)S(1)}, bf16[1,64,128]{2,1,0:T(8,128)(2,1)S(1)}, u32[]{:S(2)}, u32[]{:S(2)}) collective-permute-start(bf16[1,64,128]{2,1,0:T(8,128)(2,1)S(1)} %get-tuple-element.60), channel_id=1, source_target_pairs={{0,4},{4,8},{8,12},{12,16},{16,20},{20,24},{24,28},{1,5},{5,9},{9,... | collective-permute-start | bytes 49160 | tf_op jit(solution)/shard_map/ppermute | solution.py:15
  160.3 0.2 slice.210
  160.5 1.2 collective-permute-done.6
  161.7 1.3 copy-done.4
  (53 shorter events, 1.5 us)
Async XLA Ops:
  0.6 101.5 %copy-start = (bf16[512,256]{1,0:T(8,128)(2,1)S(1)}, bf16[512,256]{1,0:T(8,128)(2,1)}, u32[]{:S(2)}) copy-start(bf16[512,256]{1,0:T(8,128)(2,1)} %param.30) | copy-start | bytes 786436
  0.6 30.3 %copy-start.5 = (bf16[64,64,128]{2,1,0:T(8,128)(2,1)S(1)}, bf16[64,64,128]{2,1,0:T(8,128)(2,1)}, u32[]{:S(2)}) copy-start(bf16[64,64,128]{2,1,0:T(8,128)(2,1)} %param.26) | copy-start | bytes 3145732
  1.5 29.4 %collective-permute-start = (bf16[1,64,128]{2,1,0:T(8,128)(2,1)S(1)}, bf16[1,64,128]{2,1,0:T(8,128)(2,1)S(1)}, u32[]{:S(2)}, u32[]{:S(2)}) collective-permute-start(bf16[1,64,128]{2,1,0:T(8,128)(2,1)S(1)} %get-tuple-element.65), channel_id=1, source_target_pairs={{0,4},{4,8},{8,12},{12,16},{16,20},{20,24},{24,28},{1,5},{5,9},{9,... | collective-permute-start | bytes 49160 | tf_op jit(solution)/shard_map/ppermute | solution.py:15
  24.7 15.7 %all-to-all-start = ((bf16[32,2,256]{2,1,0:T(2,128)(2,1)}), bf16[32,2,256]{2,1,0:T(2,128)(2,1)S(1)}, u32[]{:S(2)}, u32[]{:S(2)}) async-start(bf16[32,2,256]{2,1,0:T(2,128)(2,1)} %reshape.210), calls=%async_computation | async-start | bytes 65536 | tf_op jit(solution)/shard_map/all_to_all | solution.py:59
  29.6 5.6 %collective-permute-start.1 = (bf16[1,64,128]{2,1,0:T(8,128)(2,1)S(1)}, bf16[1,64,128]{2,1,0:T(8,128)(2,1)S(1)}, u32[]{:S(2)}, u32[]{:S(2)}) collective-permute-start(bf16[1,64,128]{2,1,0:T(8,128)(2,1)S(1)} %get-tuple-element.64), channel_id=1, source_target_pairs={{4,0},{8,4},{12,8},{16,12},{20,16},{24,20},{28,24},{5,1},{9,5},{13... | collective-permute-start | bytes 49160 | tf_op jit(solution)/shard_map/ppermute | solution.py:17
  35.3 2.3 %collective-permute-start.3 = (bf16[66,1,128]{2,1,0:T(2,128)(2,1)S(1)}, bf16[66,1,128]{2,1,0:T(2,128)(2,1)S(1)}, u32[]{:S(2)}, u32[]{:S(2)}) collective-permute-start(bf16[66,1,128]{2,1,0:T(2,128)(2,1)S(1)} %get-tuple-element.63), channel_id=1, source_target_pairs={{1,0},{2,1},{3,2},{0,3},{5,4},{6,5},{7,6},{4,7},{9,8},{10,9},{11,1... | collective-permute-start | bytes 50696 | tf_op jit(solution)/shard_map/ppermute | solution.py:17
  36.0 3.4 %collective-permute-start.2 = (bf16[66,1,128]{2,1,0:T(2,128)(2,1)S(1)}, bf16[66,1,128]{2,1,0:T(2,128)(2,1)S(1)}, u32[]{:S(2)}, u32[]{:S(2)}) collective-permute-start(bf16[66,1,128]{2,1,0:T(2,128)(2,1)S(1)} %get-tuple-element.62), channel_id=1, source_target_pairs={{0,1},{1,2},{2,3},{3,0},{4,5},{5,6},{6,7},{7,4},{8,9},{9,10},{10,1... | collective-permute-start | bytes 50696 | tf_op jit(solution)/shard_map/ppermute | solution.py:15
  71.0 6.8 %copy-start.2 = (bf16[2048,4480]{1,0:T(8,128)(2,1)}, bf16[2048,4480]{1,0:T(8,128)(2,1)S(1)}, u32[]{:S(2)}) copy-start(bf16[2048,4480]{1,0:T(8,128)(2,1)S(1)} %fusion.4) | copy-start | bytes 55050244
  77.8 20.7 %all-to-all-start.1 = ((bf16[32,64,128]{2,1,0:T(8,128)(2,1)}), bf16[32,64,128]{2,1,0:T(8,128)(2,1)S(1)}, u32[]{:S(2)}, u32[]{:S(2)}) async-start(bf16[32,64,128]{2,1,0:T(8,128)(2,1)} %bitcast.11), calls=%async_computation.1 | async-start | bytes 1048576 | tf_op jit(solution)/shard_map/all_to_all | solution.py:88
  95.9 5.8 %copy-start.6 = (bf16[128,512]{1,0:T(8,128)(2,1)S(1)}, bf16[128,512]{1,0:T(8,128)(2,1)}, u32[]{:S(2)}) copy-start(bf16[128,512]{1,0:T(8,128)(2,1)} %param.28) | copy-start | bytes 393220
  98.5 3.7 %copy-start.7 = (f32[512]{0:T(512)S(1)}, f32[512]{0:T(512)}, u32[]{:S(2)}) copy-start(f32[512]{0:T(512)} %param.29) | copy-start | bytes 6148
  98.5 3.7 %copy-start.8 = (f32[256]{0:T(256)S(1)}, f32[256]{0:T(256)}, u32[]{:S(2)}) copy-start(f32[256]{0:T(256)} %param.31) | copy-start | bytes 3076
  98.5 3.7 %copy-start.9 = (f32[256]{0:T(256)S(1)}, f32[256]{0:T(256)}, u32[]{:S(2)}) copy-start(f32[256]{0:T(256)} %param.27) | copy-start | bytes 3076
  101.7 1.2 copy-start.10
  141.6 4.4 %copy-start.3 = (bf16[66,66,128]{2,1,0:T(8,128)(2,1)}, bf16[66,66,128]{2,1,0:T(8,128)(2,1)S(1)}, u32[]{:S(2)}) copy-start(bf16[66,66,128]{2,1,0:T(8,128)(2,1)S(1)} %convert_element_type.90) | copy-start | bytes 3345412
  141.6 2.8 %collective-permute-start.5 = (bf16[66,1,128]{2,1,0:T(2,128)(2,1)S(1)}, bf16[66,1,128]{2,1,0:T(2,128)(2,1)S(1)}, u32[]{:S(2)}, u32[]{:S(2)}) collective-permute-start(bf16[66,1,128]{2,1,0:T(2,128)(2,1)S(1)} %get-tuple-element.59), channel_id=1, source_target_pairs={{1,0},{2,1},{3,2},{0,3},{5,4},{6,5},{7,6},{4,7},{9,8},{10,9},{11,1... | collective-permute-start | bytes 50696 | tf_op jit(solution)/shard_map/ppermute | solution.py:17
  142.6 3.4 %collective-permute-start.4 = (bf16[66,1,128]{2,1,0:T(2,128)(2,1)S(1)}, bf16[66,1,128]{2,1,0:T(2,128)(2,1)S(1)}, u32[]{:S(2)}, u32[]{:S(2)}) collective-permute-start(bf16[66,1,128]{2,1,0:T(2,128)(2,1)S(1)} %get-tuple-element.58), channel_id=1, source_target_pairs={{0,1},{1,2},{2,3},{3,0},{4,5},{5,6},{6,7},{7,4},{8,9},{9,10},{10,1... | collective-permute-start | bytes 50696 | tf_op jit(solution)/shard_map/ppermute | solution.py:15
  152.4 7.8 %copy-start.1 = (f32[66,64,128]{2,1,0:T(8,128)S(1)}, f32[66,64,128]{2,1,0:T(8,128)}, u32[]{:S(2)}) copy-start(f32[66,64,128]{2,1,0:T(8,128)} %scatter-add.15) | copy-start | bytes 6488068
  154.4 6.1 %collective-permute-start.7 = (bf16[1,64,128]{2,1,0:T(8,128)(2,1)S(1)}, bf16[1,64,128]{2,1,0:T(8,128)(2,1)S(1)}, u32[]{:S(2)}, u32[]{:S(2)}) collective-permute-start(bf16[1,64,128]{2,1,0:T(8,128)(2,1)S(1)} %get-tuple-element.61), channel_id=1, source_target_pairs={{4,0},{8,4},{12,8},{16,12},{20,16},{24,20},{28,24},{5,1},{9,5},{13... | collective-permute-start | bytes 49160 | tf_op jit(solution)/shard_map/ppermute | solution.py:17
  155.7 6.0 %collective-permute-start.6 = (bf16[1,64,128]{2,1,0:T(8,128)(2,1)S(1)}, bf16[1,64,128]{2,1,0:T(8,128)(2,1)S(1)}, u32[]{:S(2)}, u32[]{:S(2)}) collective-permute-start(bf16[1,64,128]{2,1,0:T(8,128)(2,1)S(1)} %get-tuple-element.60), channel_id=1, source_target_pairs={{0,4},{4,8},{8,12},{12,16},{16,20},{20,24},{24,28},{1,5},{5,9},{9,... | collective-permute-start | bytes 49160 | tf_op jit(solution)/shard_map/ppermute | solution.py:15
  161.7 1.3 copy-start.4
where the time goes:
time: 164 us; the launch traced here: 163 us
  other arithmetic  47.7 us (29%)
  matrix products  34.3 us (21%)
  local copies, waits for them, and re-layouts  24.7 us (15%)
  starting transfers between devices  23.9 us (15%)
  blocking collectives  18.4 us (11%)
  waiting for transfers between devices  13 us (8%)
    add x1, other arithmetic, per_device(): matrix + jnp.where(indices[k][:, None] == cell_ids, weights_low[:, k:k +...  30.2 us
    all_to_all x1, blocking collectives, per_device(): lax.all_to_all(send_grad.reshape(devices, capacity, levels).astype(jnp.bf...  18.4 us
    dot_general x1, matrix products, per_device(): jnp.dot(spectra, pc_basis, preferred_element_type=jnp.float32)  12.7 us
    dot_general x1, matrix products, per_device(): lax.dot_general(matrix.astype(jnp.float32), g_owner, (((0,), (0,)), ((),...  10.2 us
    ppermute x4, starting transfers between devices, padded(): lax.ppermute(tail, axis, [(i, (i + 1) % count) for i in range(ends)])  9.38 us
    another operation x3, other arithmetic  9.15 us
    dot_general x1, matrix products, per_device(): jnp.dot(matrix, flat_pad, preferred_element_type=jnp.float32)  6.82 us
    ppermute x4, waiting for transfers between devices, padded(): lax.ppermute(head, axis, [((i + 1) % count, i) for i in range(ends)])  5.86 us
  transfers between devices with their start and end apart: 10, of which 7 were waited for; matrix products, arithmetic and copies ran while one was open for 21% of the time, Pallas kernels for 0%

commit v1 on v0

v1 whole, which is shorter than its diff:
```python
import functools

import jax
import jax.numpy as jnp
from jax import lax
from jax.experimental import pallas as pl
from jax.experimental.pallas import tpu as pltpu
from jax.sharding import PartitionSpec as P

MESH = pl.DeviceIdType.MESH
BF = jnp.bfloat16
F32 = jnp.float32
LANES = 128


def dot(a, b, dims=((1,), (0,))):
    return lax.dot_general(a, b, (dims, ((), ())), preferred_element_type=F32)


def rim_table(R, C):
    own = R * C
    ns, west, east = own, own + LANES, own + 2 * LANES
    tall = R + 16
    return [
        (-1, 0, 0, ns, C),
        (1, 0, (R - 1) * C, ns + C, C),
        (0, -1, None, east, tall),
        (0, 1, None, west + 16, tall),
        (-1, -1, 0, east + 112, 16),
        (-1, 1, C - 16, west + 112, 16),
        (1, -1, (R - 1) * C, east + 96, 16),
        (1, 1, own - 16, west + 96, 16),
    ]


def kernel(
    n_lat, n_lon, cap, R, C,
    meta_ref, state_hbm, spectra_hbm, basis_hbm, w_in_ref, b_in_ref, w_out_ref, b_out_ref, inv_ref,
    dep_hbm, grad_hbm,
    spectra_v, basis_v, pcs_v, onehot, send_meta, recv_meta, rows_v, f_sl, q_sl, f_ls, q_ls,
    cells, edges, column, pulled, g_send, g_recv, dep_slot, dep_v, total, rim_in,
    in_sem, state_sem, out_sem,
    meta_send, meta_recv, halo_send, halo_recv, col_send, col_recv, grad_send, grad_recv,
    rim_send, rim_recv,
):
    n = n_lat * n_lon
    lat = lax.axis_index("lat")
    lon = lax.axis_index("lon")
    me = lat * n_lon + lon
    slots = n * cap
    G = 256
    per = G // cap
    groups = slots // G
    mine = me // per
    own = R * C
    chunks = cells.shape[0] // LANES
    obs = meta_ref.shape[1]
    parts = obs // G
    table = rim_table(R, C)

    def at(peer):
        return (peer // n_lon, lax.rem(peer, n_lon))

    def near(dl, dc):
        return (lax.rem(lat + dl + n_lat, n_lat), lax.rem(lon + dc + n_lon, n_lon))

    barrier = pltpu.get_barrier_semaphore()

    def greet(j, carry):
        peer = lax.rem(me + j, n)
        pl.semaphore_signal(barrier, inc=1, device_id=at(peer), device_id_type=MESH)
        return carry

    lax.fori_loop(1, n, greet, 0)

    state_copy = pltpu.make_async_copy(state_hbm, cells.at[pl.ds(0, own)], state_sem)
    state_copy.start()
    basis_copy = pltpu.make_async_copy(basis_hbm, basis_v, in_sem.at[parts])
    basis_copy.start()

    def spectra_copy(i):
        rows = pl.ds(i * G, G)
        return pltpu.make_async_copy(spectra_hbm.at[rows], spectra_v.at[rows], in_sem.at[i])

    for i in range(parts):
        spectra_copy(i).start()

    dest = meta_ref[6:7, :]
    before = lax.broadcasted_iota(jnp.int32, (LANES, LANES), 0)
    after = lax.broadcasted_iota(jnp.int32, (LANES, LANES), 1)
    upto = jnp.where(before <= after, 1.0, 0.0).astype(BF)
    tile_id = lax.broadcasted_iota(jnp.int32, (n, LANES), 0).astype(F32)
    carry = jnp.zeros((n, 1), F32)
    places = []
    for b in range(obs // LANES):
        d = dest[:, b * LANES : (b + 1) * LANES]
        oh = jnp.where(tile_id == d, 1.0, 0.0)
        rank = dot(oh.astype(BF), upto) + carry
        slot = jnp.sum(rank * oh, axis=0, keepdims=True) - 1.0
        places.append(d * cap + slot)
        carry = carry + jnp.sum(oh, axis=1, keepdims=True)
    place = jnp.concatenate(places, axis=1)
    meta = meta_ref[...].astype(BF)

    def pack(g, carry):
        ids = (lax.broadcasted_iota(jnp.int32, (G, obs), 0) + g * G).astype(F32)
        sel = jnp.where(ids == place, 1.0, 0.0).astype(BF)
        onehot[pl.ds(g * G, G), :] = sel
        res = dot(meta, sel, ((1,), (1,)))
        for i in range(per):
            piece = res[:, i * cap : (i + 1) * cap]
            send_meta[g * per + i] = jnp.concatenate(
                [piece, jnp.zeros((8, LANES - cap), F32)], axis=1
            )
        return carry

    lax.fori_loop(0, groups, pack, 0)

    pl.semaphore_wait(barrier, n - 1)

    def push_meta(j, carry):
        peer = lax.rem(me + j, n)
        pltpu.make_async_remote_copy(
            src_ref=send_meta.at[peer],
            dst_ref=recv_meta.at[me],
            send_sem=meta_send,
            recv_sem=meta_recv,
            device_id=at(peer),
            device_id_type=MESH,
        ).start()
        return carry

    lax.fori_loop(1, n, push_meta, 0)
    self_meta = pltpu.make_async_copy(send_meta.at[me], recv_meta.at[me], meta_recv)
    self_meta.start()

    west0 = own + LANES
    cells[pl.ds(west0, 16), :] = jnp.zeros((16, LANES), BF)
    cells[pl.ds(west0 + LANES + 80, 16), :] = jnp.zeros((16, LANES), BF)
    state_copy.wait()
    tall = R + 16
    row = lax.broadcasted_iota(jnp.int32, (tall, own), 0)
    cell = lax.broadcasted_iota(jnp.int32, (tall, own), 1)
    cut = R - 16
    row = jnp.where(row < cut, row, jnp.where(row < R, -R, row - 16))
    for s, c in ((0, 0), (1, C - 1)):
        pick = jnp.where(cell == row * C + c, 1.0, 0.0).astype(BF)
        edges[s] = dot(pick, cells[pl.ds(0, own), :]).astype(BF)

    def halo(k):
        dl, dc, src, dst, rows = table[k]
        if src is None:
            source = edges.at[0 if dc < 0 else 1]
        else:
            source = cells.at[pl.ds(src, rows)]
        return pltpu.make_async_remote_copy(
            src_ref=source,
            dst_ref=cells.at[pl.ds(dst, rows)],
            send_sem=halo_send.at[k],
            recv_sem=halo_recv.at[k],
            device_id=near(dl, dc),
            device_id_type=MESH,
        )

    for k in range(8):
        halo(k).start()

    def components(i, carry):
        spectra_copy(i).wait()
        rows = pl.ds(i * G, G)
        pcs_v[rows, :] = dot(spectra_v[rows, :], basis_v[...]).astype(BF)
        return carry

    basis_copy.wait()
    half = parts // 2
    lax.fori_loop(0, half, components, 0)

    pltpu.make_async_copy(recv_meta, recv_meta, meta_recv).wait()
    for s in range(n):
        rows_v[:, s * cap : (s + 1) * cap] = recv_meta[s][:, 0:cap]

    def spread(g, carry):
        rows = pl.ds(pl.multiple_of(g * G, G), G)
        m = rows_v[:, rows]
        r0 = m[4:5].astype(jnp.int32) - 1
        c0 = m[5:6].astype(jnp.int32) - 1
        level = lax.broadcasted_iota(jnp.int32, (LANES, G), 0)
        f = jnp.zeros((LANES, G), F32)
        q = jnp.full((LANES, G), -1.0, F32)
        for k, (dr, dc) in enumerate(((0, 0), (1, 0), (0, 1), (1, 1))):
            r, c = r0 + dr, c0 + dc
            north, south = r < 0, r >= R
            on_w, on_e = c < 0, c >= C
            chunk = jnp.where(
                on_w, chunks - 2,
                jnp.where(on_e, chunks - 1, jnp.where(north | south, chunks - 3, r >> 1)),
            )
            low = r + jnp.where(r >= cut, 16, 0)
            lane_w = jnp.where(north, 111, jnp.where(south, 127, 16 + low))
            lane_e = jnp.where(north, 96, jnp.where(south, 112, low))
            lane = jnp.where(on_w, lane_w, jnp.where(on_e, lane_e, (r & 1) * C + c))
            outside = (north & (lat == 0)) | (south & (lat == n_lat - 1))
            w = jnp.where(outside, 0.0, m[k : k + 1])
            hit = level == lane
            f = jnp.where(hit, w, f)
            q = jnp.where(hit, chunk.astype(F32), q)
        f_ls[:, rows] = f.astype(BF)
        q_ls[:, rows] = q.astype(BF)
        f_sl[pl.ds(g * G, G), :] = f.T.astype(BF)
        q_sl[pl.ds(g * G, G), :] = q.T.astype(BF)
        return carry

    lax.fori_loop(0, groups, spread, 0)
    for k in range(8):
        halo(k).wait_recv()

    def offset(s):
        odd = lax.rem(s, 2)
        step = (s + 1) // 2
        return lax.rem(groups // 2 + step * (1 - 2 * odd) + groups, groups)

    def push(peer, src, dst, send_sem, recv_sem):
        there = pl.ds(me * cap, cap)
        here = pl.ds(peer * cap, cap)

        @pl.when(peer != me)
        def _():
            pltpu.make_async_remote_copy(
                src_ref=src.at[here],
                dst_ref=dst.at[there],
                send_sem=send_sem,
                recv_sem=recv_sem,
                device_id=at(peer),
                device_id_type=MESH,
            ).start()

        @pl.when(peer == me)
        def _():
            pltpu.make_async_copy(src.at[here], dst.at[there], recv_sem).start()

    def interpolate(s, carry):
        g = lax.rem(mine + offset(s), groups)
        rows = pl.ds(g * G, G)
        f, q = f_sl[rows, :], q_sl[rows, :]
        zero = jnp.zeros((G, LANES), BF)
        matrix = jnp.concatenate(
            [jnp.where(q == jnp.array(ch, BF), f, zero) for ch in range(chunks)], axis=1
        )
        column[rows, :] = dot(matrix, cells[...]).astype(BF)
        for i in range(per):
            push(g * per + i, column, pulled, col_send, col_recv.at[mine])
        return carry

    lax.fori_loop(0, groups, interpolate, 0)

    lax.fori_loop(half, parts, components, 0)

    def network(s, carry):
        g = lax.rem(mine - offset(s) + groups, groups)
        rows = pl.ds(g * G, G)
        pltpu.make_async_copy(pulled.at[rows], pulled.at[rows], col_recv.at[g]).wait()
        pre = dot(pulled[rows, :], w_in_ref[...]) + b_in_ref[...]
        sig = jax.nn.sigmoid(pre)
        hidden = (pre * sig).astype(BF)
        sim = dot(hidden, w_out_ref[...]) + b_out_ref[...]
        pcs = dot(onehot[rows, :], pcs_v[...])
        inv = inv_ref[...]
        dep = (sim - pcs) * inv
        dep_slot[rows, :] = dep.astype(BF)
        g_sim = (dep * inv).astype(BF)
        g_hidden = dot(g_sim, w_out_ref[...], ((1,), (1,)))
        g_pre = (g_hidden * sig * (1.0 + pre * (1.0 - sig))).astype(BF)
        g_send[rows, :] = dot(g_pre, w_in_ref[...], ((1,), (1,))).astype(BF)
        for i in range(per):
            push(g * per + i, g_send, g_recv, grad_send, grad_recv.at[mine])
        return carry

    lax.fori_loop(0, groups, network, 0)

    def ordered(i, carry):
        sel = onehot[:, pl.ds(pl.multiple_of(i * G, G), G)]
        dep_v[pl.ds(i * G, G), :] = dot(sel, dep_slot[...], ((0,), (0,))).astype(BF)
        return carry

    lax.fori_loop(0, parts, ordered, 0)
    dep_copy = pltpu.make_async_copy(dep_v, dep_hbm, out_sem.at[0])
    dep_copy.start()

    total[...] = jnp.zeros_like(total)
    block = 7

    def accumulate(s, carry):
        g = lax.rem(mine + offset(s), groups)
        lanes = pl.ds(pl.multiple_of(g * G, G), G)
        rows = pl.ds(g * G, G)
        pltpu.make_async_copy(g_recv.at[rows], g_recv.at[rows], grad_recv.at[g]).wait()
        f, q = f_ls[:, lanes], q_ls[:, lanes]
        zero = jnp.zeros((LANES, G), BF)
        x = g_recv[rows, :]
        for b in range(0, chunks, block):
            last = min(b + block, chunks)
            matrix = jnp.concatenate(
                [jnp.where(q == jnp.array(ch, BF), f, zero) for ch in range(b, last)], axis=0
            )
            total[b * LANES : last * LANES, :] += dot(matrix, x)
        return carry

    lax.fori_loop(0, groups, accumulate, 0)

    starts, at_row = [], 0
    for k in range(8):
        starts.append(at_row)
        at_row += table[k][4]

    def rim(k):
        dl, dc, src, dst, rows = table[k]
        return pltpu.make_async_remote_copy(
            src_ref=total.at[pl.ds(dst, rows)],
            dst_ref=rim_in.at[pl.ds(starts[k], rows)],
            send_sem=rim_send.at[k],
            recv_sem=rim_recv.at[k],
            device_id=near(-dl, -dc),
            device_id_type=MESH,
        )

    for k in range(8):
        rim(k).start()
    for k in range(8):
        rim(k).wait_recv()
    for k in range(8):
        dl, dc, src, dst, rows = table[k]
        if src is not None:
            total[src : src + rows, :] += rim_in[starts[k] : starts[k] + rows, :]
        else:
            first = 0 if dc < 0 else C - 1
            got = rim_in[starts[k] : starts[k] + rows, :]
            got = jnp.concatenate([got[0:cut], got[R : R + 16]], axis=0)
            there = pl.ds(first, R, stride=C)
            total[there, :] = total[there, :] + got
    grad_copy = pltpu.make_async_copy(total.at[pl.ds(0, own)], grad_hbm, out_sem.at[1])
    grad_copy.start()

    for k in range(8):
        halo(k).wait_send()
        rim(k).wait_send()

    def sent(ref, count, sem):
        part = ref.at[pl.ds(0, count)]
        pltpu.make_async_remote_copy(
            src_ref=part, dst_ref=part, send_sem=sem, recv_sem=sem,
            device_id=near(0, 1), device_id_type=MESH,
        ).wait_send()

    sent(send_meta, n - 1, meta_send)
    sent(column, (n - 1) * cap, col_send)
    sent(g_send, (n - 1) * cap, grad_send)
    dep_copy.wait()
    grad_copy.wait()


def per_device(
    n_lat, n_lon,
    spectra, pc_basis, destination, corner_row, corner_col, corner_weight, state, inv_sigma,
    w_in, b_in, w_out, b_out,
):
    n = n_lat * n_lon
    obs, channels = spectra.shape
    R, C, levels = state.shape
    comps = pc_basis.shape[1]
    cap = max(2, 2 * obs // n)
    slots = n * cap
    own = R * C
    ncell = own + 3 * LANES
    assert 2 * C == LANES and R == C and levels == LANES and slots % 256 == 0 and obs % 256 == 0
    meta = jnp.concatenate(
        [
            corner_weight.astype(F32).T,
            corner_row.astype(F32)[None, :],
            corner_col.astype(F32)[None, :],
            destination.astype(F32).T,
            jnp.zeros((1, obs), F32),
        ],
        axis=0,
    )
    vm = pl.BlockSpec(memory_space=pltpu.VMEM)
    hbm = pl.BlockSpec(memory_space=pl.ANY)
    dma = pltpu.SemaphoreType.DMA
    rim_rows = sum(t[4] for t in rim_table(R, C))
    dep, grad = pl.pallas_call(
        functools.partial(kernel, n_lat, n_lon, cap, R, C),
        out_shape=(
            jax.ShapeDtypeStruct((obs, comps), BF),
            jax.ShapeDtypeStruct((own, levels), F32),
        ),
        in_specs=[vm, hbm, hbm, hbm, vm, vm, vm, vm, vm],
        out_specs=(hbm, hbm),
        scratch_shapes=[
            pltpu.VMEM((obs, channels), BF),
            pltpu.VMEM((channels, comps), BF),
            pltpu.VMEM((obs, comps), BF),
            pltpu.VMEM((slots, obs), BF),
            pltpu.VMEM((n, 8, LANES), F32),
            pltpu.VMEM((n, 8, LANES), F32),
            pltpu.VMEM((8, slots), F32),
            pltpu.VMEM((slots, LANES), BF),
            pltpu.VMEM((slots, LANES), BF),
            pltpu.VMEM((LANES, slots), BF),
            pltpu.VMEM((LANES, slots), BF),
            pltpu.VMEM((ncell, levels), BF),
            pltpu.VMEM((2, R + 16, levels), BF),
            pltpu.VMEM((slots, levels), BF),
            pltpu.VMEM((slots, levels), BF),
            pltpu.VMEM((slots, levels), BF),
            pltpu.VMEM((slots, levels), BF),
            pltpu.VMEM((slots, comps), BF),
            pltpu.VMEM((obs, comps), BF),
            pltpu.VMEM((ncell, levels), F32),
            pltpu.VMEM((rim_rows, levels), F32),
            dma((obs // 256 + 1,)),
            dma,
            dma((2,)),
            dma, dma, dma((8,)), dma((8,)),
            dma, dma((slots // 256,)), dma, dma((slots // 256,)),
            dma((8,)), dma((8,)),
        ],
        compiler_params=pltpu.CompilerParams(
            collective_id=0, has_side_effects=True, vmem_limit_bytes=56 * 1024 * 1024
        ),
    )(
        meta, state.reshape(own, levels), spectra, pc_basis,
        w_in, b_in[None, :], w_out, b_out[None, :], inv_sigma[None, :],
    )
    return dep, grad.reshape(R, C, levels)


def solution(mesh):
    n_lat, n_lon = mesh.shape["lat"], mesh.shape["lon"]
    return jax.shard_map(
        functools.partial(per_device, n_lat, n_lon),
        mesh=mesh,
        in_specs=(
            P(("lat", "lon"), None),
            P(),
            P(("lat", "lon"), None),
            P(("lat", "lon")),
            P(("lat", "lon")),
            P(("lat", "lon"), None),
            P("lat", "lon", None),
            P(),
            P(),
            P(),
            P(),
            P(),
        ),
        out_specs=(P(("lat", "lon"), None), P("lat", "lon", None)),
        check_vma=False,
    )
```

time: 164 us -> 60 us (0.37)
  Pallas kernels: 0 us -> 50.1 us
  other arithmetic: 47.7 us -> 2.77 us
  matrix products: 34.3 us -> 0 us
  starting transfers between devices: 23.9 us -> 0 us
  local copies, waits for them, and re-layouts: 24.7 us -> 5.68 us
  blocking collectives: 18.4 us -> 0 us
  waiting for transfers between devices: 13 us -> 0 us
    pallas_call x0 -> x1, Pallas kernels: none -> 50.1 us  [per_device(): pl.pallas_call(functools.partial(kernel, n_lat, n_lon, cap, R, C), out_sh...]
    dot_general x6 -> x0, matrix products: 34.3 us -> none  [the longest x1 12.7 us: per_device(): jnp.dot(spectra, pc_basis, preferred_element_type=jnp.float32)]
    add x4 -> x0, other arithmetic: 31.5 us -> none  [the longest x1 30.2 us: per_device(): matrix + jnp.where(indices[k][:, None] == cell_ids, weights_low[:, k:k +...]
    all_to_all x1 -> x0, blocking collectives: 18.4 us -> none  [per_device(): lax.all_to_all(send_grad.reshape(devices, capacity, levels).astype(jnp.bf...]
    ppermute x8 -> x0, starting transfers between devices: 13.7 us -> none  [the longest x4 9.38 us: padded(): lax.ppermute(tail, axis, [(i, (i + 1) % count) for i in range(ends)])]
    ppermute x8 -> x0, waiting for transfers between devices: 10.4 us -> none  [the longest x4 5.86 us: padded(): lax.ppermute(head, axis, [((i + 1) % count, i) for i in range(ends)])]
    all_to_all x2 -> x0, starting transfers between devices: 10.2 us -> none  [the longest x1 5.31 us: per_device(): lax.all_to_all(column.reshape(devices, capacity, levels), ('lat', 'lon'),...]
    another operation x3 -> x0, other arithmetic: 9.15 us -> none
  transfers between devices with their start and end apart: 10 -> 0, of which waited for: 7 -> 0; matrix products, arithmetic and copies ran while one was open for 21% -> 0% of each run, Pallas kernels for 0% -> 0%
where the time goes in v1:
time: 60 us; the launch traced here: 59.1 us
  Pallas kernels  50.1 us (84%)
  local copies, waits for them, and re-layouts  5.68 us (9%)
  other arithmetic  2.77 us (5%)
  between operations  0.64 us (1%)
    pallas_call x1, Pallas kernels, per_device(): pl.pallas_call(functools.partial(kernel, n_lat, n_lon, cap, R, C), out_sh...  50.1 us
    unnamed x2, local copies, waits for them, and re-layouts  5.03 us

profile of v1, /device:TPU:0, one launch (start us, length us, event | category | flops | bytes accessed | tf_op | source)
XLA Modules:
  0.0 59.1 jit_solution(12548134111143228982)
XLA Ops:
  0.6 0.7 %convert_bitcast_fusion.1 = f32[1,1024]{1,0:T(1,128)S(1)} fusion(s32[1024,1]{0,1:T(1,128)} %param.14), kind=kLoop, calls=%fused_computation.1 | loop fusion | flops 1024 | bytes 8192 | tf_op jit(solution)/shard_map/transpose | solution.py:380
  1.3 0.7 %convert_element_type.10 = f32[1024]{0:T(1024)S(1)} convert(s32[1024]{0:T(1024)} %param.15) | non-fusion elementwise | flops 1024 | bytes 8192 | tf_op jit(solution)/shard_map/convert_element_type | solution.py:378
  2.0 0.7 %convert_element_type.11 = f32[1024]{0:T(1024)S(1)} convert(s32[1024]{0:T(1024)} %param.16) | non-fusion elementwise | flops 1024 | bytes 8192 | tf_op jit(solution)/shard_map/convert_element_type | solution.py:379
  2.7 0.7 %convert_bitcast_fusion = f32[4,1024]{1,0:T(4,128)S(1)} fusion(bf16[1024,4]{0,1:T(4,128)(2,1)} %param.17), kind=kLoop, calls=%fused_computation | loop fusion | flops 4096 | bytes 24576 | tf_op jit(solution)/shard_map/transpose | solution.py:377
  3.4 0.6 %concatenate.3.meta_ref = f32[8,1024]{1,0:T(8,128)} concatenate(f32[4,1024]{1,0:T(4,128)S(1)} %convert_bitcast_fusion, f32[1,1024]{1,0:T(1,128)S(1)} %bitcast.13, f32[1,1024]{1,0:T(1,128)S(1)} %bitcast.14, f32[1,1024]{1,0:T(1,128)S(1)} %convert_bitcast_fusion.1, f32[1,1024]{1,0:T(1,128)S(1)} %broadcast_in_dim.20), dimensions={0} | concatenate | bytes 65536 | tf_op jit(solution)/shard_map/concatenate | solution.py:375
  4.1 50.1 %shard_map.131 = (bf16[1024,256]{1,0:T(8,128)(2,1)}, f32[4096,128]{1,0:T(8,128)}) custom-call(f32[8,1024]{1,0:T(8,128)} %concatenate.3.meta_ref, bf16[4096,128]{1,0:T(8,128)(2,1)} %bitcast.12, bf16[1024,8448]{1,0:T(8,128)(2,1)} %spectra_hbm.1, bf16[8448,256]{1,0:T(8,128)(2,1)} %basis_hbm.1, bf16[128,512]{1,0:T(8,128)(2,1)} %w_in_ref.1, f32[1,512]{1,0:T(1,128)} %bitcast.15, ...), custom_call_target="tpu_custom_call" | custom-call | tf_op jit(solution)/shard_map/pallas_call | solution.py:389
  54.1 1.9 %copy.16 = bf16[1024,256]{1,0:T(8,128)(2,1)} copy(bf16[1024,256]{1,0:T(8,128)(2,1)} %get-tuple-element.8) | data formatting | bytes 1048576
  56.0 3.2 %copy.17 = f32[64,64,128]{2,1,0:T(8,128)} copy(f32[64,64,128]{2,1,0:T(8,128)} %bitcast.11) | data formatting | bytes 4194304
  (1 shorter events, 0.0 us)

commit v2 on v1

--- a/solution.py
+++ b/solution.py
@@ -35,11 +35,11 @@
 
 def kernel(
     n_lat, n_lon, cap, R, C,
-    meta_ref, state_hbm, spectra_hbm, basis_hbm, w_in_ref, b_in_ref, w_out_ref, b_out_ref, inv_ref,
-    dep_hbm, grad_hbm,
-    spectra_v, basis_v, pcs_v, onehot, send_meta, recv_meta, rows_v, f_sl, q_sl, f_ls, q_ls,
-    cells, edges, column, pulled, g_send, g_recv, dep_slot, dep_v, total, rim_in,
-    in_sem, state_sem, out_sem,
+    dest_ref, row_ref, col_ref, weight_ref, state_hbm, spectra_hbm, basis_hbm, w_in_ref, b_in_ref, w_out_ref, b_out_ref, inv_ref,
+    dep_ref, grad_ref,
+    meta_ref, spectra_v, basis_v, pcs_v, onehot, send_meta, recv_meta, rows_v, f_sl, q_sl, f_ls, q_ls,
+    cells, edges, column, pulled, g_send, g_recv, dep_slot, rim_out, rim_in,
+    in_sem, state_sem,
     meta_send, meta_recv, halo_send, halo_recv, col_send, col_recv, grad_send, grad_recv,
     rim_send, rim_recv,
 ):
@@ -85,7 +85,11 @@
     for i in range(parts):
         spectra_copy(i).start()
 
-    dest = meta_ref[6:7, :]
+    dest = dest_ref[...].astype(F32)
+    meta_ref[0:4, :] = weight_ref[...].astype(F32)
+    meta_ref[4:5, :] = row_ref[...].astype(F32)
+    meta_ref[5:6, :] = col_ref[...].astype(F32)
+    meta_ref[6:8, :] = jnp.zeros((2, obs), F32)
     before = lax.broadcasted_iota(jnp.int32, (LANES, LANES), 0)
     after = lax.broadcasted_iota(jnp.int32, (LANES, LANES), 1)
     upto = jnp.where(before <= after, 1.0, 0.0).astype(BF)
@@ -172,7 +176,7 @@
         return carry
 
     basis_copy.wait()
-    half = parts // 2
+    half = 1
     lax.fori_loop(0, half, components, 0)
 
     pltpu.make_async_copy(recv_meta, recv_meta, meta_recv).wait()
@@ -279,30 +283,38 @@
 
     def ordered(i, carry):
         sel = onehot[:, pl.ds(pl.multiple_of(i * G, G), G)]
-        dep_v[pl.ds(i * G, G), :] = dot(sel, dep_slot[...], ((0,), (0,))).astype(BF)
+        dep_ref[pl.ds(i * G, G), :] = dot(sel, dep_slot[...], ((0,), (0,))).astype(BF)
         return carry
 
     lax.fori_loop(0, parts, ordered, 0)
-    dep_copy = pltpu.make_async_copy(dep_v, dep_hbm, out_sem.at[0])
-    dep_copy.start()
-
-    total[...] = jnp.zeros_like(total)
-    block = 7
-
-    def accumulate(s, carry):
+
+    grad_ref[...] = jnp.zeros_like(grad_ref)
+    rim_out[...] = jnp.zeros_like(rim_out)
+    block = 8
+
+    def add_chunks(s, into, first, stop):
         g = lax.rem(mine + offset(s), groups)
         lanes = pl.ds(pl.multiple_of(g * G, G), G)
-        rows = pl.ds(g * G, G)
-        pltpu.make_async_copy(g_recv.at[rows], g_recv.at[rows], grad_recv.at[g]).wait()
         f, q = f_ls[:, lanes], q_ls[:, lanes]
         zero = jnp.zeros((LANES, G), BF)
-        x = g_recv[rows, :]
-        for b in range(0, chunks, block):
-            last = min(b + block, chunks)
+        x = g_recv[pl.ds(g * G, G), :]
+        for b in range(first, stop, block):
+            last = min(b + block, stop)
             matrix = jnp.concatenate(
                 [jnp.where(q == jnp.array(ch, BF), f, zero) for ch in range(b, last)], axis=0
             )
-            total[b * LANES : last * LANES, :] += dot(matrix, x)
+            into[(b - first) * LANES : (last - first) * LANES, :] += dot(matrix, x)
+
+    def accumulate(s, carry):
+        g = lax.rem(mine + offset(s), groups)
+        rows = pl.ds(g * G, G)
+        pltpu.make_async_copy(g_recv.at[rows], g_recv.at[rows], grad_recv.at[g]).wait()
+        add_chunks(s, rim_out, chunks - 3, chunks)
+
+        @pl.when(s < groups - 1)
+        def _():
+            add_chunks(s, grad_ref, 0, chunks - 3)
+
         return carry
 
     lax.fori_loop(0, groups, accumulate, 0)
@@ -315,7 +327,7 @@
     def rim(k):
         dl, dc, src, dst, rows = table[k]
         return pltpu.make_async_remote_copy(
-            src_ref=total.at[pl.ds(dst, rows)],
+            src_ref=rim_out.at[pl.ds(dst - own, rows)],
             dst_ref=rim_in.at[pl.ds(starts[k], rows)],
             send_sem=rim_send.at[k],
             recv_sem=rim_recv.at[k],
@@ -325,20 +337,19 @@
 
     for k in range(8):
         rim(k).start()
+    add_chunks(groups - 1, grad_ref, 0, chunks - 3)
     for k in range(8):
         rim(k).wait_recv()
     for k in range(8):
         dl, dc, src, dst, rows = table[k]
         if src is not None:
-            total[src : src + rows, :] += rim_in[starts[k] : starts[k] + rows, :]
+            grad_ref[src : src + rows, :] += rim_in[starts[k] : starts[k] + rows, :]
         else:
             first = 0 if dc < 0 else C - 1
             got = rim_in[starts[k] : starts[k] + rows, :]
             got = jnp.concatenate([got[0:cut], got[R : R + 16]], axis=0)
             there = pl.ds(first, R, stride=C)
-            total[there, :] = total[there, :] + got
-    grad_copy = pltpu.make_async_copy(total.at[pl.ds(0, own)], grad_hbm, out_sem.at[1])
-    grad_copy.start()
+            grad_ref[there, :] = grad_ref[there, :] + got
 
     for k in range(8):
         halo(k).wait_send()
@@ -354,8 +365,6 @@
     sent(send_meta, n - 1, meta_send)
     sent(column, (n - 1) * cap, col_send)
     sent(g_send, (n - 1) * cap, grad_send)
-    dep_copy.wait()
-    grad_copy.wait()
 
 
 def per_device(
@@ -372,16 +381,6 @@
     own = R * C
     ncell = own + 3 * LANES
     assert 2 * C == LANES and R == C and levels == LANES and slots % 256 == 0 and obs % 256 == 0
-    meta = jnp.concatenate(
-        [
-            corner_weight.astype(F32).T,
-            corner_row.astype(F32)[None, :],
-            corner_col.astype(F32)[None, :],
-            destination.astype(F32).T,
-            jnp.zeros((1, obs), F32),
-        ],
-        axis=0,
-    )
     vm = pl.BlockSpec(memory_space=pltpu.VMEM)
     hbm = pl.BlockSpec(memory_space=pl.ANY)
     dma = pltpu.SemaphoreType.DMA
@@ -392,9 +391,10 @@
             jax.ShapeDtypeStruct((obs, comps), BF),
             jax.ShapeDtypeStruct((own, levels), F32),
         ),
-        in_specs=[vm, hbm, hbm, hbm, vm, vm, vm, vm, vm],
-        out_specs=(hbm, hbm),
+        in_specs=[vm, vm, vm, vm, hbm, hbm, hbm, vm, vm, vm, vm, vm],
+        out_specs=(vm, vm),
         scratch_shapes=[
+            pltpu.VMEM((8, obs), F32),
             pltpu.VMEM((obs, channels), BF),
             pltpu.VMEM((channels, comps), BF),
             pltpu.VMEM((obs, comps), BF),
@@ -413,21 +413,20 @@
             pltpu.VMEM((slots, levels), BF),
             pltpu.VMEM((slots, levels), BF),
             pltpu.VMEM((slots, comps), BF),
-            pltpu.VMEM((obs, comps), BF),
-            pltpu.VMEM((ncell, levels), F32),
+            pltpu.VMEM((3 * LANES, levels), F32),
             pltpu.VMEM((rim_rows, levels), F32),
             dma((obs // 256 + 1,)),
             dma,
-            dma((2,)),
             dma, dma, dma((8,)), dma((8,)),
             dma, dma((slots // 256,)), dma, dma((slots // 256,)),
             dma((8,)), dma((8,)),
         ],
         compiler_params=pltpu.CompilerParams(
-            collective_id=0, has_side_effects=True, vmem_limit_bytes=56 * 1024 * 1024
+            collective_id=0, has_side_effects=True, vmem_limit_bytes=46 * 1024 * 1024
         ),
     )(
-        meta, state.reshape(own, levels), spectra, pc_basis,
+        destination.T, corner_row[None, :], corner_col[None, :], corner_weight.T,
+        state.reshape(own, levels), spectra, pc_basis,
         w_in, b_in[None, :], w_out, b_out[None, :], inv_sigma[None, :],
     )
     return dep, grad.reshape(R, C, levels)

time: 60 us -> 59.4 us (0.990)
  local copies, waits for them, and re-layouts: 5.68 us -> 9.98 us
  other arithmetic: 2.77 us -> 0 us
  Pallas kernels: 50.1 us -> 48.1 us
    unnamed x2 -> x22, local copies, waits for them, and re-layouts: 5.03 us -> 9.98 us
    pallas_call x1, Pallas kernels: 50.1 us -> 48.1 us  [per_device(): pl.pallas_call(functools.partial(kernel, n_lat, n_lon, cap, R, C), out_sh...]
    transpose x2 -> x0, other arithmetic: 1.39 us -> none  [the longest x1 0.7 us: per_device(): corner_weight.astype(F32)]
    convert_element_type x2 -> x0, other arithmetic: 1.38 us -> none  [the longest x1 0.69 us: per_device(): corner_row.astype(F32)[None, :]]
    concatenate x1 -> x0, local copies, waits for them, and re-layouts: 0.65 us -> none  [per_device(): jnp.concatenate([corner_weight.astype(F32).T, corner_row.astype(F32)[None...]
where the time goes in v2:
time: 59.4 us; the launch traced here: 58.8 us
  Pallas kernels  48.1 us (81%)
  local copies, waits for them, and re-layouts  9.98 us (17%)
  between operations  0.66 us (1%)
    pallas_call x1, Pallas kernels, per_device(): pl.pallas_call(functools.partial(kernel, n_lat, n_lon, cap, R, C), out_sh...  48.1 us
    unnamed x22, local copies, waits for them, and re-layouts  9.98 us

profile of v2, /device:TPU:0, one launch (start us, length us, event | category | flops | bytes accessed | tf_op | source)
XLA Modules:
  0.0 58.8 jit_solution(10920295867050639778)
XLA Ops:
  0.6 0.0 copy-start
  0.6 1.2 %copy-done = bf16[64,64,128]{2,1,0:T(8,128)(2,1)S(1)} copy-done((bf16[64,64,128]{2,1,0:T(8,128)(2,1)S(1)}, bf16[64,64,128]{2,1,0:T(8,128)(2,1)}, u32[]{:S(2)}) %copy-start) | copy-done | bytes 1048600
  1.9 0.0 copy-start.1
  1.9 0.9 %copy-done.1 = bf16[512,256]{1,0:T(8,128)(2,1)S(1)} copy-done((bf16[512,256]{1,0:T(8,128)(2,1)S(1)}, bf16[512,256]{1,0:T(8,128)(2,1)}, u32[]{:S(2)}) %copy-start.1) | copy-done | bytes 262168
  2.8 0.0 copy-start.2
  2.8 0.9 %copy-done.2 = bf16[128,512]{1,0:T(8,128)(2,1)S(1)} copy-done((bf16[128,512]{1,0:T(8,128)(2,1)S(1)}, bf16[128,512]{1,0:T(8,128)(2,1)}, u32[]{:S(2)}) %copy-start.2) | copy-done | bytes 131096
  3.7 0.0 copy-start.3
  3.7 0.7 %copy-done.3 = bf16[1024,4]{0,1:T(4,128)(2,1)S(1)} copy-done((bf16[1024,4]{0,1:T(4,128)(2,1)S(1)}, bf16[1024,4]{0,1:T(4,128)(2,1)}, u32[]{:S(2)}) %copy-start.3) | copy-done | bytes 8216
  4.4 0.0 copy-start.4
  4.4 0.7 %copy-done.4 = s32[1024,1]{0,1:T(1,128)S(1)} copy-done((s32[1024,1]{0,1:T(1,128)S(1)}, s32[1024,1]{0,1:T(1,128)}, u32[]{:S(2)}) %copy-start.4) | copy-done | bytes 4120
  5.1 0.0 copy-start.5
  5.1 0.7 %copy-done.5 = s32[1024]{0:T(1024)S(1)} copy-done((s32[1024]{0:T(1024)S(1)}, s32[1024]{0:T(1024)}, u32[]{:S(2)}) %copy-start.5) | copy-done | bytes 4120
  5.8 0.0 copy-start.6
  5.8 0.7 %copy-done.6 = s32[1024]{0:T(1024)S(1)} copy-done((s32[1024]{0:T(1024)S(1)}, s32[1024]{0:T(1024)}, u32[]{:S(2)}) %copy-start.6) | copy-done | bytes 4120
  6.5 0.0 copy-start.7
  6.5 0.7 %copy-done.7 = f32[512]{0:T(512)S(1)} copy-done((f32[512]{0:T(512)S(1)}, f32[512]{0:T(512)}, u32[]{:S(2)}) %copy-start.7) | copy-done | bytes 2072
  7.2 0.0 copy-start.8
  7.2 0.7 %copy-done.8 = f32[256]{0:T(256)S(1)} copy-done((f32[256]{0:T(256)S(1)}, f32[256]{0:T(256)}, u32[]{:S(2)}) %copy-start.8) | copy-done | bytes 1048
  7.8 0.0 copy-start.9
  7.8 0.7 %copy-done.9 = f32[256]{0:T(256)S(1)} copy-done((f32[256]{0:T(256)S(1)}, f32[256]{0:T(256)}, u32[]{:S(2)}) %copy-start.9) | copy-done | bytes 1048
  8.5 48.1 %shard_map.131 = (bf16[1024,256]{1,0:T(8,128)(2,1)S(1)}, f32[4096,128]{1,0:T(8,128)S(1)}) custom-call(s32[1,1024]{1,0:T(1,128)S(1)} %bitcast.12, s32[1,1024]{1,0:T(1,128)S(1)} %bitcast.13, s32[1,1024]{1,0:T(1,128)S(1)} %bitcast.14, bf16[4,1024]{1,0:T(4,128)(2,1)S(1)} %bitcast.11, bf16[4096,128]{1,0:T(8,128)(2,1)S(1)} %bitcast.10, ...), custom_call_target="tpu_custom_call" | custom-call | tf_op jit(solution)/shard_map/pallas_call | solution.py:388
  56.7 0.8 %copy.16 = bf16[1024,256]{1,0:T(8,128)(2,1)} copy(bf16[1024,256]{1,0:T(8,128)(2,1)S(1)} %get-tuple-element.8) | data formatting | bytes 1048576
  57.4 1.3 %copy.17 = f32[64,64,128]{2,1,0:T(8,128)} copy(f32[64,64,128]{2,1,0:T(8,128)S(1)} %bitcast.9) | data formatting | bytes 4194304
Async XLA Ops:
  0.6 1.2 %copy-start = (bf16[64,64,128]{2,1,0:T(8,128)(2,1)S(1)}, bf16[64,64,128]{2,1,0:T(8,128)(2,1)}, u32[]{:S(2)}) copy-start(bf16[64,64,128]{2,1,0:T(8,128)(2,1)} %param.18) | copy-start | bytes 3145732
  1.9 0.9 %copy-start.1 = (bf16[512,256]{1,0:T(8,128)(2,1)S(1)}, bf16[512,256]{1,0:T(8,128)(2,1)}, u32[]{:S(2)}) copy-start(bf16[512,256]{1,0:T(8,128)(2,1)} %w_out_ref.1) | copy-start | bytes 786436
  2.8 0.9 %copy-start.2 = (bf16[128,512]{1,0:T(8,128)(2,1)S(1)}, bf16[128,512]{1,0:T(8,128)(2,1)}, u32[]{:S(2)}) copy-start(bf16[128,512]{1,0:T(8,128)(2,1)} %w_in_ref.1) | copy-start | bytes 393220
  3.7 0.7 %copy-start.3 = (bf16[1024,4]{0,1:T(4,128)(2,1)S(1)}, bf16[1024,4]{0,1:T(4,128)(2,1)}, u32[]{:S(2)}) copy-start(bf16[1024,4]{0,1:T(4,128)(2,1)} %param.17) | copy-start | bytes 24580
  4.4 0.7 %copy-start.4 = (s32[1024,1]{0,1:T(1,128)S(1)}, s32[1024,1]{0,1:T(1,128)}, u32[]{:S(2)}) copy-start(s32[1024,1]{0,1:T(1,128)} %param.14) | copy-start | bytes 12292
  5.1 0.7 %copy-start.5 = (s32[1024]{0:T(1024)S(1)}, s32[1024]{0:T(1024)}, u32[]{:S(2)}) copy-start(s32[1024]{0:T(1024)} %param.15) | copy-start | bytes 12292
  5.8 0.7 %copy-start.6 = (s32[1024]{0:T(1024)S(1)}, s32[1024]{0:T(1024)}, u32[]{:S(2)}) copy-start(s32[1024]{0:T(1024)} %param.16) | copy-start | bytes 12292
  6.5 0.7 %copy-start.7 = (f32[512]{0:T(512)S(1)}, f32[512]{0:T(512)}, u32[]{:S(2)}) copy-start(f32[512]{0:T(512)} %param.21) | copy-start | bytes 6148
  7.2 0.7 %copy-start.8 = (f32[256]{0:T(256)S(1)}, f32[256]{0:T(256)}, u32[]{:S(2)}) copy-start(f32[256]{0:T(256)} %param.23) | copy-start | bytes 3076
  7.8 0.7 %copy-start.9 = (f32[256]{0:T(256)S(1)}, f32[256]{0:T(256)}, u32[]{:S(2)}) copy-start(f32[256]{0:T(256)} %param.19) | copy-start | bytes 3076

commit v3 on v2

--- a/solution.py
+++ b/solution.py
@@ -35,11 +35,13 @@
 
 def kernel(
     n_lat, n_lon, cap, R, C,
-    dest_ref, row_ref, col_ref, weight_ref, state_hbm, spectra_hbm, basis_hbm, w_in_ref, b_in_ref, w_out_ref, b_out_ref, inv_ref,
+    dest_hbm, row_hbm, col_hbm, weight_hbm, w_in_hbm, b_in_hbm, w_out_hbm, b_out_hbm, inv_hbm,
+    state_hbm, spectra_hbm, basis_hbm,
     dep_ref, grad_ref,
+    dest_ref, row_ref, col_ref, weight_ref, w_in_ref, b_in_ref, w_out_ref, b_out_ref, inv_ref,
     meta_ref, spectra_v, basis_v, pcs_v, onehot, send_meta, recv_meta, rows_v, f_sl, q_sl, f_ls, q_ls,
     cells, edges, column, pulled, g_send, g_recv, dep_slot, rim_out, rim_in,
-    in_sem, state_sem,
+    small_sem, in_sem, state_sem,
     meta_send, meta_recv, halo_send, halo_recv, col_send, col_recv, grad_send, grad_recv,
     rim_send, rim_recv,
 ):
@@ -64,15 +66,18 @@
     def near(dl, dc):
         return (lax.rem(lat + dl + n_lat, n_lat), lax.rem(lon + dc + n_lon, n_lon))
 
-    barrier = pltpu.get_barrier_semaphore()
-
-    def greet(j, carry):
-        peer = lax.rem(me + j, n)
-        pl.semaphore_signal(barrier, inc=1, device_id=at(peer), device_id_type=MESH)
-        return carry
-
-    lax.fori_loop(1, n, greet, 0)
-
+    small = [
+        pltpu.make_async_copy(src, dst, small_sem.at[i])
+        for i, (src, dst) in enumerate(
+            (
+                (dest_hbm, dest_ref), (row_hbm, row_ref), (col_hbm, col_ref),
+                (weight_hbm, weight_ref), (w_in_hbm, w_in_ref), (b_in_hbm, b_in_ref),
+                (w_out_hbm, w_out_ref), (b_out_hbm, b_out_ref), (inv_hbm, inv_ref),
+            )
+        )
+    ]
+    for copy in small:
+        copy.start()
     state_copy = pltpu.make_async_copy(state_hbm, cells.at[pl.ds(0, own)], state_sem)
     state_copy.start()
     basis_copy = pltpu.make_async_copy(basis_hbm, basis_v, in_sem.at[parts])
@@ -85,6 +90,17 @@
     for i in range(parts):
         spectra_copy(i).start()
 
+    barrier = pltpu.get_barrier_semaphore()
+
+    def greet(j, carry):
+        peer = lax.rem(me + j, n)
+        pl.semaphore_signal(barrier, inc=1, device_id=at(peer), device_id_type=MESH)
+        return carry
+
+    lax.fori_loop(1, n, greet, 0)
+
+    for copy in small:
+        copy.wait()
     dest = dest_ref[...].astype(F32)
     meta_ref[0:4, :] = weight_ref[...].astype(F32)
     meta_ref[4:5, :] = row_ref[...].astype(F32)
@@ -107,7 +123,7 @@
     meta = meta_ref[...].astype(BF)
 
     def pack(g, carry):
-        ids = (lax.broadcasted_iota(jnp.int32, (G, obs), 0) + g * G).astype(F32)
+        ids = (lax.broadcasted_iota(jnp.int32, (G, 1), 0) + g * G).astype(F32)
         sel = jnp.where(ids == place, 1.0, 0.0).astype(BF)
         onehot[pl.ds(g * G, G), :] = sel
         res = dot(meta, sel, ((1,), (1,)))
@@ -143,13 +159,16 @@
     cells[pl.ds(west0 + LANES + 80, 16), :] = jnp.zeros((16, LANES), BF)
     state_copy.wait()
     tall = R + 16
-    row = lax.broadcasted_iota(jnp.int32, (tall, own), 0)
-    cell = lax.broadcasted_iota(jnp.int32, (tall, own), 1)
     cut = R - 16
+    line = lax.broadcasted_iota(jnp.int32, (2 * tall, 1), 0)
+    side = jnp.where(line < tall, 0, 1)
+    row = line - side * tall
     row = jnp.where(row < cut, row, jnp.where(row < R, -R, row - 16))
-    for s, c in ((0, 0), (1, C - 1)):
-        pick = jnp.where(cell == row * C + c, 1.0, 0.0).astype(BF)
-        edges[s] = dot(pick, cells[pl.ds(0, own), :]).astype(BF)
+    cell = lax.broadcasted_iota(jnp.int32, (2 * tall, own), 1)
+    pick = jnp.where(cell == row * C + side * (C - 1), 1.0, 0.0).astype(BF)
+    both = dot(pick, cells[pl.ds(0, own), :]).astype(BF)
+    edges[0] = both[0:tall]
+    edges[1] = both[tall:]
 
     def halo(k):
         dl, dc, src, dst, rows = table[k]
@@ -259,27 +278,38 @@
 
     lax.fori_loop(half, parts, components, 0)
 
-    def network(s, carry):
-        g = lax.rem(mine - offset(s) + groups, groups)
+    def group(g):
         rows = pl.ds(g * G, G)
-        pltpu.make_async_copy(pulled.at[rows], pulled.at[rows], col_recv.at[g]).wait()
         pre = dot(pulled[rows, :], w_in_ref[...]) + b_in_ref[...]
-        sig = jax.nn.sigmoid(pre)
-        hidden = (pre * sig).astype(BF)
-        sim = dot(hidden, w_out_ref[...]) + b_out_ref[...]
+        sig = 0.5 * jnp.tanh(0.5 * pre) + 0.5
+        hid = pre * sig
+        sim = dot(hid.astype(BF), w_out_ref[...]) + b_out_ref[...]
         pcs = dot(onehot[rows, :], pcs_v[...])
         inv = inv_ref[...]
         dep = (sim - pcs) * inv
         dep_slot[rows, :] = dep.astype(BF)
         g_sim = (dep * inv).astype(BF)
         g_hidden = dot(g_sim, w_out_ref[...], ((1,), (1,)))
-        g_pre = (g_hidden * sig * (1.0 + pre * (1.0 - sig))).astype(BF)
+        g_pre = (g_hidden * (sig + hid * (1.0 - sig))).astype(BF)
         g_send[rows, :] = dot(g_pre, w_in_ref[...], ((1,), (1,))).astype(BF)
-        for i in range(per):
-            push(g * per + i, g_send, g_recv, grad_send, grad_recv.at[mine])
-        return carry
-
-    lax.fori_loop(0, groups, network, 0)
+
+    together = 2 if groups % 2 == 0 else 1
+
+    def network(s, carry):
+        order = [
+            lax.rem(mine - offset(s * together + t) + groups, groups) for t in range(together)
+        ]
+        for g in order:
+            rows = pl.ds(g * G, G)
+            pltpu.make_async_copy(pulled.at[rows], pulled.at[rows], col_recv.at[g]).wait()
+        for g in order:
+            group(g)
+        for g in order:
+            for i in range(per):
+                push(g * per + i, g_send, g_recv, grad_send, grad_recv.at[mine])
+        return carry
+
+    lax.fori_loop(0, groups // together, network, 0)
 
     def ordered(i, carry):
         sel = onehot[:, pl.ds(pl.multiple_of(i * G, G), G)]
@@ -382,18 +412,27 @@
     ncell = own + 3 * LANES
     assert 2 * C == LANES and R == C and levels == LANES and slots % 256 == 0 and obs % 256 == 0
     vm = pl.BlockSpec(memory_space=pltpu.VMEM)
-    hbm = pl.BlockSpec(memory_space=pl.ANY)
+    hbm = pl.BlockSpec(memory_space=pltpu.HBM)
     dma = pltpu.SemaphoreType.DMA
     rim_rows = sum(t[4] for t in rim_table(R, C))
     dep, grad = pl.pallas_call(
         functools.partial(kernel, n_lat, n_lon, cap, R, C),
         out_shape=(
-            jax.ShapeDtypeStruct((obs, comps), BF),
-            jax.ShapeDtypeStruct((own, levels), F32),
+            pltpu.VMEM((obs, comps), BF),
+            pltpu.VMEM((own, levels), F32),
         ),
-        in_specs=[vm, vm, vm, vm, hbm, hbm, hbm, vm, vm, vm, vm, vm],
+        in_specs=[hbm] * 12,
         out_specs=(vm, vm),
         scratch_shapes=[
+            pltpu.VMEM((1, obs), jnp.int32),
+            pltpu.VMEM((1, obs), jnp.int32),
+            pltpu.VMEM((1, obs), jnp.int32),
+            pltpu.VMEM((4, obs), BF),
+            pltpu.VMEM(w_in.shape, BF),
+            pltpu.VMEM((1, b_in.shape[0]), F32),
+            pltpu.VMEM(w_out.shape, BF),
+            pltpu.VMEM((1, comps), F32),
+            pltpu.VMEM((1, comps), F32),
             pltpu.VMEM((8, obs), F32),
             pltpu.VMEM((obs, channels), BF),
             pltpu.VMEM((channels, comps), BF),
@@ -415,6 +454,7 @@
             pltpu.VMEM((slots, comps), BF),
             pltpu.VMEM((3 * LANES, levels), F32),
             pltpu.VMEM((rim_rows, levels), F32),
+            dma((9,)),
             dma((obs // 256 + 1,)),
             dma,
             dma, dma, dma((8,)), dma((8,)),
@@ -422,12 +462,12 @@
             dma((8,)), dma((8,)),
         ],
         compiler_params=pltpu.CompilerParams(
-            collective_id=0, has_side_effects=True, vmem_limit_bytes=46 * 1024 * 1024
+            collective_id=0, has_side_effects=True, vmem_limit_bytes=58 * 1024 * 1024
         ),
     )(
         destination.T, corner_row[None, :], corner_col[None, :], corner_weight.T,
+        w_in, b_in[None, :], w_out, b_out[None, :], inv_sigma[None, :],
         state.reshape(own, levels), spectra, pc_basis,
-        w_in, b_in[None, :], w_out, b_out[None, :], inv_sigma[None, :],
     )
     return dep, grad.reshape(R, C, levels)
 

time: 59.4 us -> 57.1 us (0.961)
  local copies, waits for them, and re-layouts: 9.98 us -> 2.11 us
  Pallas kernels: 48.1 us -> 54.1 us
    unnamed x22 -> x2, local copies, waits for them, and re-layouts: 9.98 us -> 2.11 us
    pallas_call x1, Pallas kernels: 48.1 us -> 54.1 us  [per_device(): pl.pallas_call(functools.partial(kernel, n_lat, n_lon, cap, R, C), out_sh...]
where the time goes in v3:
time: 57.1 us; the launch traced here: 56.9 us
  Pallas kernels  54.1 us (95%)
  local copies, waits for them, and re-layouts  2.11 us (4%)
  between operations  0.64 us (1%)
    pallas_call x1, Pallas kernels, per_device(): pl.pallas_call(functools.partial(kernel, n_lat, n_lon, cap, R, C), out_sh...  54.1 us
    unnamed x2, local copies, waits for them, and re-layouts  2.11 us

profile of v3, /device:TPU:0, one launch (start us, length us, event | category | flops | bytes accessed | tf_op | source)
XLA Modules:
  0.0 56.9 jit_solution(17047349488546458288)
XLA Ops:
  0.6 54.1 %shard_map.131 = (bf16[1024,256]{1,0:T(8,128)(2,1)S(1)}, f32[4096,128]{1,0:T(8,128)S(1)}) custom-call(s32[1,1024]{1,0:T(1,128)} %bitcast.12, s32[1,1024]{1,0:T(1,128)} %bitcast.13, s32[1,1024]{1,0:T(1,128)} %bitcast.14, bf16[4,1024]{1,0:T(4,128)(2,1)} %bitcast.11, bf16[128,512]{1,0:T(8,128)(2,1)} %w_in_hbm.1, f32[1,512]{1,0:T(1,128)} %bitcast.15, ...), custom_call_target="tpu_custom_call" | custom-call | tf_op jit(solution)/shard_map/pallas_call | solution.py:418
  54.7 0.8 %copy.16 = bf16[1024,256]{1,0:T(8,128)(2,1)} copy(bf16[1024,256]{1,0:T(8,128)(2,1)S(1)} %get-tuple-element.6) | data formatting | bytes 1048576
  55.5 1.3 %copy.17 = f32[64,64,128]{2,1,0:T(8,128)} copy(f32[64,64,128]{2,1,0:T(8,128)S(1)} %bitcast.9) | data formatting | bytes 4194304

commit v4 on v3

--- a/solution.py
+++ b/solution.py
@@ -39,7 +39,7 @@
     state_hbm, spectra_hbm, basis_hbm,
     dep_ref, grad_ref,
     dest_ref, row_ref, col_ref, weight_ref, w_in_ref, b_in_ref, w_out_ref, b_out_ref, inv_ref,
-    meta_ref, spectra_v, basis_v, pcs_v, onehot, send_meta, recv_meta, rows_v, f_sl, q_sl, f_ls, q_ls,
+    meta_ref, spectra_v, basis_v, pcs_v, onehot, send_meta, recv_meta, f_ls, q_ls,
     cells, edges, column, pulled, g_send, g_recv, dep_slot, rim_out, rim_in,
     small_sem, in_sem, state_sem,
     meta_send, meta_recv, halo_send, halo_recv, col_send, col_recv, grad_send, grad_recv,
@@ -102,10 +102,13 @@
     for copy in small:
         copy.wait()
     dest = dest_ref[...].astype(F32)
-    meta_ref[0:4, :] = weight_ref[...].astype(F32)
-    meta_ref[4:5, :] = row_ref[...].astype(F32)
-    meta_ref[5:6, :] = col_ref[...].astype(F32)
-    meta_ref[6:8, :] = jnp.zeros((2, obs), F32)
+    weights = weight_ref[...].astype(F32)
+    for k, line in enumerate((0, 4, 1, 5)):
+        meta_ref[line : line + 1, :] = weights[k : k + 1]
+    meta_ref[2:3, :] = row_ref[...].astype(F32)
+    meta_ref[6:7, :] = col_ref[...].astype(F32)
+    meta_ref[3:4, :] = jnp.zeros((1, obs), F32)
+    meta_ref[7:8, :] = jnp.zeros((1, obs), F32)
     before = lax.broadcasted_iota(jnp.int32, (LANES, LANES), 0)
     after = lax.broadcasted_iota(jnp.int32, (LANES, LANES), 1)
     upto = jnp.where(before <= after, 1.0, 0.0).astype(BF)
@@ -122,37 +125,29 @@
     place = jnp.concatenate(places, axis=1)
     meta = meta_ref[...].astype(BF)
 
-    def pack(g, carry):
-        ids = (lax.broadcasted_iota(jnp.int32, (G, 1), 0) + g * G).astype(F32)
-        sel = jnp.where(ids == place, 1.0, 0.0).astype(BF)
-        onehot[pl.ds(g * G, G), :] = sel
-        res = dot(meta, sel, ((1,), (1,)))
-        for i in range(per):
-            piece = res[:, i * cap : (i + 1) * cap]
-            send_meta[g * per + i] = jnp.concatenate(
-                [piece, jnp.zeros((8, LANES - cap), F32)], axis=1
-            )
-        return carry
-
-    lax.fori_loop(0, groups, pack, 0)
-
-    pl.semaphore_wait(barrier, n - 1)
-
-    def push_meta(j, carry):
-        peer = lax.rem(me + j, n)
-        pltpu.make_async_remote_copy(
-            src_ref=send_meta.at[peer],
-            dst_ref=recv_meta.at[me],
-            send_sem=meta_send,
-            recv_sem=meta_recv,
-            device_id=at(peer),
-            device_id_type=MESH,
-        ).start()
-        return carry
-
-    lax.fori_loop(1, n, push_meta, 0)
-    self_meta = pltpu.make_async_copy(send_meta.at[me], recv_meta.at[me], meta_recv)
-    self_meta.start()
+    def offset(s):
+        odd = lax.rem(s, 2)
+        step = (s + 1) // 2
+        return lax.rem(groups // 2 + step * (1 - 2 * odd) + groups, groups)
+
+    def push(peer, source, target, send_sem, recv_sem):
+        @pl.when(peer != me)
+        def _():
+            pltpu.make_async_remote_copy(
+                src_ref=source,
+                dst_ref=target,
+                send_sem=send_sem,
+                recv_sem=recv_sem,
+                device_id=at(peer),
+                device_id_type=MESH,
+            ).start()
+
+        @pl.when(peer == me)
+        def _():
+            pltpu.make_async_copy(source, target, recv_sem).start()
+
+    def slots_of(device):
+        return pl.ds(device * cap, cap)
 
     west0 = own + LANES
     cells[pl.ds(west0, 16), :] = jnp.zeros((16, LANES), BF)
@@ -185,28 +180,45 @@
             device_id_type=MESH,
         )
 
+    pl.semaphore_wait(barrier, n - 1)
     for k in range(8):
         halo(k).start()
 
-    def components(i, carry):
-        spectra_copy(i).wait()
-        rows = pl.ds(i * G, G)
-        pcs_v[rows, :] = dot(spectra_v[rows, :], basis_v[...]).astype(BF)
-        return carry
-
-    basis_copy.wait()
-    half = 1
-    lax.fori_loop(0, half, components, 0)
-
-    pltpu.make_async_copy(recv_meta, recv_meta, meta_recv).wait()
-    for s in range(n):
-        rows_v[:, s * cap : (s + 1) * cap] = recv_meta[s][:, 0:cap]
-
-    def spread(g, carry):
-        rows = pl.ds(pl.multiple_of(g * G, G), G)
-        m = rows_v[:, rows]
-        r0 = m[4:5].astype(jnp.int32) - 1
-        c0 = m[5:6].astype(jnp.int32) - 1
+    def pack(s, carry):
+        g = lax.rem(mine - offset(s) + groups, groups)
+        ids = (lax.broadcasted_iota(jnp.int32, (G, 1), 0) + g * G).astype(F32)
+        sel = jnp.where(ids == place, 1.0, 0.0).astype(BF)
+        onehot[pl.ds(g * G, G), :] = sel
+        res = dot(meta, sel, ((1,), (1,)))
+        for i in range(per):
+            lanes = slice(i * cap, (i + 1) * cap)
+            piece = [res[0:4, lanes], res[4:8, lanes]]
+            if 2 * cap < LANES:
+                piece.append(jnp.zeros((4, LANES - 2 * cap), F32))
+            send_meta[g * per + i] = jnp.concatenate(piece, axis=1)
+        for i in range(per):
+            peer = g * per + i
+            push(
+                peer, send_meta.at[peer], recv_meta.at[me], meta_send, meta_recv.at[mine]
+            )
+        return carry
+
+    lax.fori_loop(0, groups, pack, 0)
+
+    for k in range(8):
+        halo(k).wait_recv()
+
+    def interpolate(s, carry):
+        g = lax.rem(mine + offset(s), groups)
+        devices = pl.ds(g * per, per)
+        pltpu.make_async_copy(
+            recv_meta.at[devices], recv_meta.at[devices], meta_recv.at[g]
+        ).wait()
+        got = [recv_meta[g * per + i] for i in range(per)]
+        top = jnp.concatenate([x[:, 0:cap] for x in got], axis=1)
+        low_half = jnp.concatenate([x[:, cap : 2 * cap] for x in got], axis=1)
+        r0 = top[2:3].astype(jnp.int32) - 1
+        c0 = low_half[2:3].astype(jnp.int32) - 1
         level = lax.broadcasted_iota(jnp.int32, (LANES, G), 0)
         f = jnp.zeros((LANES, G), F32)
         q = jnp.full((LANES, G), -1.0, F32)
@@ -223,60 +235,39 @@
             lane_e = jnp.where(north, 96, jnp.where(south, 112, low))
             lane = jnp.where(on_w, lane_w, jnp.where(on_e, lane_e, (r & 1) * C + c))
             outside = (north & (lat == 0)) | (south & (lat == n_lat - 1))
-            w = jnp.where(outside, 0.0, m[k : k + 1])
+            weight = (top, low_half)[k % 2][k // 2 : k // 2 + 1]
+            w = jnp.where(outside, 0.0, weight)
             hit = level == lane
             f = jnp.where(hit, w, f)
             q = jnp.where(hit, chunk.astype(F32), q)
-        f_ls[:, rows] = f.astype(BF)
-        q_ls[:, rows] = q.astype(BF)
-        f_sl[pl.ds(g * G, G), :] = f.T.astype(BF)
-        q_sl[pl.ds(g * G, G), :] = q.T.astype(BF)
-        return carry
-
-    lax.fori_loop(0, groups, spread, 0)
-    for k in range(8):
-        halo(k).wait_recv()
-
-    def offset(s):
-        odd = lax.rem(s, 2)
-        step = (s + 1) // 2
-        return lax.rem(groups // 2 + step * (1 - 2 * odd) + groups, groups)
-
-    def push(peer, src, dst, send_sem, recv_sem):
-        there = pl.ds(me * cap, cap)
-        here = pl.ds(peer * cap, cap)
-
-        @pl.when(peer != me)
-        def _():
-            pltpu.make_async_remote_copy(
-                src_ref=src.at[here],
-                dst_ref=dst.at[there],
-                send_sem=send_sem,
-                recv_sem=recv_sem,
-                device_id=at(peer),
-                device_id_type=MESH,
-            ).start()
-
-        @pl.when(peer == me)
-        def _():
-            pltpu.make_async_copy(src.at[here], dst.at[there], recv_sem).start()
-
-    def interpolate(s, carry):
-        g = lax.rem(mine + offset(s), groups)
-        rows = pl.ds(g * G, G)
-        f, q = f_sl[rows, :], q_sl[rows, :]
+        lanes = pl.ds(pl.multiple_of(g * G, G), G)
+        f_ls[:, lanes] = f.astype(BF)
+        q_ls[:, lanes] = q.astype(BF)
+        f = f.T.astype(BF)
+        q = q.T.astype(BF)
         zero = jnp.zeros((G, LANES), BF)
         matrix = jnp.concatenate(
             [jnp.where(q == jnp.array(ch, BF), f, zero) for ch in range(chunks)], axis=1
         )
-        column[rows, :] = dot(matrix, cells[...]).astype(BF)
+        column[pl.ds(g * G, G), :] = dot(matrix, cells[...]).astype(BF)
         for i in range(per):
-            push(g * per + i, column, pulled, col_send, col_recv.at[mine])
+            peer = g * per + i
+            push(
+                peer, column.at[slots_of(peer)], pulled.at[slots_of(me)],
+                col_send, col_recv.at[mine],
+            )
         return carry
 
     lax.fori_loop(0, groups, interpolate, 0)
 
-    lax.fori_loop(half, parts, components, 0)
+    def components(i, carry):
+        spectra_copy(i).wait()
+        rows = pl.ds(i * G, G)
+        pcs_v[rows, :] = dot(spectra_v[rows, :], basis_v[...]).astype(BF)
+        return carry
+
+    basis_copy.wait()
+    lax.fori_loop(0, parts, components, 0)
 
     def group(g):
         rows = pl.ds(g * G, G)
@@ -306,7 +297,11 @@
             group(g)
         for g in order:
             for i in range(per):
-                push(g * per + i, g_send, g_recv, grad_send, grad_recv.at[mine])
+                peer = g * per + i
+                push(
+                    peer, g_send.at[slots_of(peer)], g_recv.at[slots_of(me)],
+                    grad_send, grad_recv.at[mine],
+                )
         return carry
 
     lax.fori_loop(0, groups // together, network, 0)
@@ -438,11 +433,8 @@
             pltpu.VMEM((channels, comps), BF),
             pltpu.VMEM((obs, comps), BF),
             pltpu.VMEM((slots, obs), BF),
-            pltpu.VMEM((n, 8, LANES), F32),
-            pltpu.VMEM((n, 8, LANES), F32),
-            pltpu.VMEM((8, slots), F32),
-            pltpu.VMEM((slots, LANES), BF),
-            pltpu.VMEM((slots, LANES), BF),
+            pltpu.VMEM((n, 4, LANES), F32),
+            pltpu.VMEM((n, 4, LANES), F32),
             pltpu.VMEM((LANES, slots), BF),
             pltpu.VMEM((LANES, slots), BF),
             pltpu.VMEM((ncell, levels), BF),
@@ -457,7 +449,7 @@
             dma((9,)),
             dma((obs // 256 + 1,)),
             dma,
-            dma, dma, dma((8,)), dma((8,)),
+            dma, dma((slots // 256,)), dma((8,)), dma((8,)),
             dma, dma((slots // 256,)), dma, dma((slots // 256,)),
             dma((8,)), dma((8,)),
         ],

time: 57.1 us -> 54.6 us (0.956)
  Pallas kernels: 54.1 us -> 51.7 us
    pallas_call x1, Pallas kernels: 54.1 us -> 51.7 us  [per_device(): pl.pallas_call(functools.partial(kernel, n_lat, n_lon, cap, R, C), out_sh...]
where the time goes in v4:
time: 54.6 us; the launch traced here: 54.4 us
  Pallas kernels  51.7 us (95%)
  local copies, waits for them, and re-layouts  2.11 us (4%)
  between operations  0.64 us (1%)
    pallas_call x1, Pallas kernels, per_device(): pl.pallas_call(functools.partial(kernel, n_lat, n_lon, cap, R, C), out_sh...  51.7 us
    unnamed x2, local copies, waits for them, and re-layouts  2.11 us

profile of v4, /device:TPU:0, one launch (start us, length us, event | category | flops | bytes accessed | tf_op | source)
XLA Modules:
  0.0 54.4 jit_solution(7219851222911381009)
XLA Ops:
  0.6 51.7 %shard_map.131 = (bf16[1024,256]{1,0:T(8,128)(2,1)S(1)}, f32[4096,128]{1,0:T(8,128)S(1)}) custom-call(s32[1,1024]{1,0:T(1,128)} %bitcast.12, s32[1,1024]{1,0:T(1,128)} %bitcast.13, s32[1,1024]{1,0:T(1,128)} %bitcast.14, bf16[4,1024]{1,0:T(4,128)(2,1)} %bitcast.11, bf16[128,512]{1,0:T(8,128)(2,1)} %w_in_hbm.1, f32[1,512]{1,0:T(1,128)} %bitcast.15, ...), custom_call_target="tpu_custom_call" | custom-call | tf_op jit(solution)/shard_map/pallas_call | solution.py:413
  52.3 0.8 %copy.16 = bf16[1024,256]{1,0:T(8,128)(2,1)} copy(bf16[1024,256]{1,0:T(8,128)(2,1)S(1)} %get-tuple-element.6) | data formatting | bytes 1048576
  53.1 1.3 %copy.17 = f32[64,64,128]{2,1,0:T(8,128)} copy(f32[64,64,128]{2,1,0:T(8,128)S(1)} %bitcast.9) | data formatting | bytes 4194304

commit v5 on v4

--- a/solution.py
+++ b/solution.py
@@ -40,7 +40,7 @@
     dep_ref, grad_ref,
     dest_ref, row_ref, col_ref, weight_ref, w_in_ref, b_in_ref, w_out_ref, b_out_ref, inv_ref,
     meta_ref, spectra_v, basis_v, pcs_v, onehot, send_meta, recv_meta, f_ls, q_ls,
-    cells, edges, column, pulled, g_send, g_recv, dep_slot, rim_out, rim_in,
+    cells, wide, edges, in_lower, column, pulled, g_send, g_recv, dep_slot, rim_out, rim_in,
     small_sem, in_sem, state_sem,
     meta_send, meta_recv, halo_send, halo_recv, col_send, col_recv, grad_send, grad_recv,
     rim_send, rim_recv,
@@ -55,7 +55,8 @@
     groups = slots // G
     mine = me // per
     own = R * C
-    chunks = cells.shape[0] // LANES
+    side_chunks = own // 2 // LANES
+    chunks = side_chunks + 4
     obs = meta_ref.shape[1]
     parts = obs // G
     table = rim_table(R, C)
@@ -207,6 +208,13 @@
 
     for k in range(8):
         halo(k).wait_recv()
+    middle = own // 2
+    wide[0:middle, 0:LANES] = cells[0:middle, :]
+    wide[0:middle, LANES:] = cells[middle:own, :]
+    wide[middle : middle + LANES, 0:LANES] = cells[middle : middle + LANES, :]
+    wide[middle : middle + LANES, LANES:] = jnp.zeros((LANES, LANES), BF)
+    wide[middle + LANES :, 0:LANES] = cells[own:, :]
+    wide[middle + LANES :, LANES:] = cells[own:, :]
 
     def interpolate(s, carry):
         g = lax.rem(mine + offset(s), groups)
@@ -219,6 +227,7 @@
         low_half = jnp.concatenate([x[:, cap : 2 * cap] for x in got], axis=1)
         r0 = top[2:3].astype(jnp.int32) - 1
         c0 = low_half[2:3].astype(jnp.int32) - 1
+        lower = jnp.where(r0 >= R // 2, 1, 0)
         level = lax.broadcasted_iota(jnp.int32, (LANES, G), 0)
         f = jnp.zeros((LANES, G), F32)
         q = jnp.full((LANES, G), -1.0, F32)
@@ -226,9 +235,10 @@
             r, c = r0 + dr, c0 + dc
             north, south = r < 0, r >= R
             on_w, on_e = c < 0, c >= C
+            inner = (r >> 1) - lower * side_chunks
             chunk = jnp.where(
                 on_w, chunks - 2,
-                jnp.where(on_e, chunks - 1, jnp.where(north | south, chunks - 3, r >> 1)),
+                jnp.where(on_e, chunks - 1, jnp.where(north | south, chunks - 3, inner)),
             )
             low = r + jnp.where(r >= cut, 16, 0)
             lane_w = jnp.where(north, 111, jnp.where(south, 127, 16 + low))
@@ -249,7 +259,12 @@
         matrix = jnp.concatenate(
             [jnp.where(q == jnp.array(ch, BF), f, zero) for ch in range(chunks)], axis=1
         )
-        column[pl.ds(g * G, G), :] = dot(matrix, cells[...]).astype(BF)
+        low = jnp.broadcast_to(lower.astype(F32), (LANES, G)).T
+        in_lower[pl.ds(g * G, G), :] = low.astype(BF)
+        both = dot(matrix, wide[...])
+        column[pl.ds(g * G, G), :] = jnp.where(
+            low > 0.5, both[:, LANES:], both[:, 0:LANES]
+        ).astype(BF)
         for i in range(per):
             peer = g * per + i
             push(
@@ -317,28 +332,48 @@
     rim_out[...] = jnp.zeros_like(rim_out)
     block = 8
 
-    def add_chunks(s, into, first, stop):
+    def products(s):
         g = lax.rem(mine + offset(s), groups)
         lanes = pl.ds(pl.multiple_of(g * G, G), G)
+        rows = pl.ds(g * G, G)
         f, q = f_ls[:, lanes], q_ls[:, lanes]
         zero = jnp.zeros((LANES, G), BF)
-        x = g_recv[pl.ds(g * G, G), :]
-        for b in range(first, stop, block):
-            last = min(b + block, stop)
+        low, x = in_lower[rows, :], g_recv[rows, :]
+        x = jnp.concatenate(
+            [jnp.where(low == jnp.array(h, BF), x, jnp.zeros_like(x)) for h in (0, 1)], axis=1
+        )
+
+        def part(first, stop):
             matrix = jnp.concatenate(
-                [jnp.where(q == jnp.array(ch, BF), f, zero) for ch in range(b, last)], axis=0
+                [jnp.where(q == jnp.array(ch, BF), f, zero) for ch in range(first, stop)], axis=0
             )
-            into[(b - first) * LANES : (last - first) * LANES, :] += dot(matrix, x)
+            return dot(matrix, x)
+
+        return part
+
+    def add_rim(s):
+        res = products(s)(side_chunks + 1, chunks)
+        rim_out[...] += res[:, 0:LANES] + res[:, LANES:]
+
+    def add_tile(s):
+        part = products(s)
+        for b in range(0, side_chunks, block):
+            last = min(b + block, side_chunks)
+            res = part(b, last)
+            grad_ref[b * LANES : last * LANES, :] += res[:, 0:LANES]
+            grad_ref[middle + b * LANES : middle + last * LANES, :] += res[:, LANES:]
+        res = part(side_chunks, side_chunks + 1)
+        grad_ref[middle : middle + LANES, :] += res[:, 0:LANES]
 
     def accumulate(s, carry):
         g = lax.rem(mine + offset(s), groups)
         rows = pl.ds(g * G, G)
         pltpu.make_async_copy(g_recv.at[rows], g_recv.at[rows], grad_recv.at[g]).wait()
-        add_chunks(s, rim_out, chunks - 3, chunks)
+        add_rim(s)
 
         @pl.when(s < groups - 1)
         def _():
-            add_chunks(s, grad_ref, 0, chunks - 3)
+            add_tile(s)
 
         return carry
 
@@ -362,7 +397,7 @@
 
     for k in range(8):
         rim(k).start()
-    add_chunks(groups - 1, grad_ref, 0, chunks - 3)
+    add_tile(groups - 1)
     for k in range(8):
         rim(k).wait_recv()
     for k in range(8):
@@ -438,7 +473,9 @@
             pltpu.VMEM((LANES, slots), BF),
             pltpu.VMEM((LANES, slots), BF),
             pltpu.VMEM((ncell, levels), BF),
+            pltpu.VMEM((own // 2 + 4 * LANES, 2 * levels), BF),
             pltpu.VMEM((2, R + 16, levels), BF),
+            pltpu.VMEM((slots, LANES), BF),
             pltpu.VMEM((slots, levels), BF),
             pltpu.VMEM((slots, levels), BF),
             pltpu.VMEM((slots, levels), BF),

time: 54.6 us -> 51.3 us (0.940)
  Pallas kernels: 51.7 us -> 48 us
    pallas_call x1, Pallas kernels: 51.7 us -> 48 us  [per_device(): pl.pallas_call(functools.partial(kernel, n_lat, n_lon, cap, R, C), out_sh...]
where the time goes in v5:
time: 51.3 us; the launch traced here: 50.8 us
  Pallas kernels  48 us (94%)
  local copies, waits for them, and re-layouts  2.11 us (4%)
  between operations  0.64 us (1%)
    pallas_call x1, Pallas kernels, per_device(): pl.pallas_call(functools.partial(kernel, n_lat, n_lon, cap, R, C), out_sh...  48 us
    unnamed x2, local copies, waits for them, and re-layouts  2.11 us

profile of v5, /device:TPU:0, one launch (start us, length us, event | category | flops | bytes accessed | tf_op | source)
XLA Modules:
  0.0 50.8 jit_solution(17920901151029226712)
XLA Ops:
  0.6 48.0 %shard_map.131 = (bf16[1024,256]{1,0:T(8,128)(2,1)S(1)}, f32[4096,128]{1,0:T(8,128)S(1)}) custom-call(s32[1,1024]{1,0:T(1,128)} %bitcast.12, s32[1,1024]{1,0:T(1,128)} %bitcast.13, s32[1,1024]{1,0:T(1,128)} %bitcast.14, bf16[4,1024]{1,0:T(4,128)(2,1)} %bitcast.11, bf16[128,512]{1,0:T(8,128)(2,1)} %w_in_hbm.1, f32[1,512]{1,0:T(1,128)} %bitcast.15, ...), custom_call_target="tpu_custom_call" | custom-call | tf_op jit(solution)/shard_map/pallas_call | solution.py:448
  48.6 0.8 %copy.16 = bf16[1024,256]{1,0:T(8,128)(2,1)} copy(bf16[1024,256]{1,0:T(8,128)(2,1)S(1)} %get-tuple-element.6) | data formatting | bytes 1048576
  49.4 1.3 %copy.17 = f32[64,64,128]{2,1,0:T(8,128)} copy(f32[64,64,128]{2,1,0:T(8,128)S(1)} %bitcast.9) | data formatting | bytes 4194304

commit v6 on v5

--- a/solution.py
+++ b/solution.py
@@ -181,6 +181,8 @@
             device_id_type=MESH,
         )
 
+    grad_ref[...] = jnp.zeros_like(grad_ref)
+    rim_out[...] = jnp.zeros_like(rim_out)
     pl.semaphore_wait(barrier, n - 1)
     for k in range(8):
         halo(k).start()
@@ -326,10 +328,9 @@
         dep_ref[pl.ds(i * G, G), :] = dot(sel, dep_slot[...], ((0,), (0,))).astype(BF)
         return carry
 
-    lax.fori_loop(0, parts, ordered, 0)
-
-    grad_ref[...] = jnp.zeros_like(grad_ref)
-    rim_out[...] = jnp.zeros_like(rim_out)
+    early = parts // 2
+    lax.fori_loop(0, early, ordered, 0)
+
     block = 8
 
     def products(s):
@@ -398,6 +399,7 @@
     for k in range(8):
         rim(k).start()
     add_tile(groups - 1)
+    lax.fori_loop(early, parts, ordered, 0)
     for k in range(8):
         rim(k).wait_recv()
     for k in range(8):

time: 51.3 us -> 51.4 us (level)
  no operation moved by 1% of the time
where the time goes in v6:
time: 51.4 us; the launch traced here: 50.9 us
  Pallas kernels  48.1 us (94%)
  local copies, waits for them, and re-layouts  2.11 us (4%)
  between operations  0.64 us (1%)
    pallas_call x1, Pallas kernels, per_device(): pl.pallas_call(functools.partial(kernel, n_lat, n_lon, cap, R, C), out_sh...  48.1 us
    unnamed x2, local copies, waits for them, and re-layouts  2.11 us

profile of v6, /device:TPU:0, one launch (start us, length us, event | category | flops | bytes accessed | tf_op | source)
XLA Modules:
  0.0 50.9 jit_solution(9276839086329758428)
XLA Ops:
  0.6 48.1 %shard_map.131 = (bf16[1024,256]{1,0:T(8,128)(2,1)S(1)}, f32[4096,128]{1,0:T(8,128)S(1)}) custom-call(s32[1,1024]{1,0:T(1,128)} %bitcast.12, s32[1,1024]{1,0:T(1,128)} %bitcast.13, s32[1,1024]{1,0:T(1,128)} %bitcast.14, bf16[4,1024]{1,0:T(4,128)(2,1)} %bitcast.11, bf16[128,512]{1,0:T(8,128)(2,1)} %w_in_hbm.1, f32[1,512]{1,0:T(1,128)} %bitcast.15, ...), custom_call_target="tpu_custom_call" | custom-call | tf_op jit(solution)/shard_map/pallas_call | solution.py:450
  48.8 0.8 %copy.16 = bf16[1024,256]{1,0:T(8,128)(2,1)} copy(bf16[1024,256]{1,0:T(8,128)(2,1)S(1)} %get-tuple-element.6) | data formatting | bytes 1048576
  49.6 1.3 %copy.17 = f32[64,64,128]{2,1,0:T(8,128)} copy(f32[64,64,128]{2,1,0:T(8,128)S(1)} %bitcast.9) | data formatting | bytes 4194304
